TPU v7x, 768 devices: a whole 4x8x12 slice. The times are simulated.
768 devices in a mesh: expert: 16 (over x, y_lo), replica: 48 (over y_hi, z, core).
Axes of the slice: x: 4, y: 8 (y_hi: 2, y_lo: 4; y = y_hi * 4 + y_lo), z: 12, core: 2. Of those that a mesh axis runs over, the one named last changes fastest.
Arguments:
- gradients: bfloat16 [48, 128, 48, 4096], P('replica', 'expert'), may hold values from -1792 to 1792
- master: float32 [128, 48, 4096], P('expert', 'replica'), may hold values from -400 to 400
- moment: float32 [128, 48, 4096], P('expert', 'replica'), may hold values from -4 to 4
- second: float32 [128, 48, 4096], P('expert', 'replica'), may hold values from 0.05 to 2
- loads: int32 [128], P('expert'), may hold values from 256 to 2047
- outlier_channels: int32 [128, 16], P('expert'), may hold values from 0 to 4095, as said below
- destination: int32 [128], P('expert'), may hold values from 0 to 127, as said below
Outputs:
- new_master: float32 [128, 48, 4096], P('expert', 'replica')
- new_moment: float32 [128, 48, 4096], P('expert', 'replica')
- new_second: float32 [128, 48, 4096], P('expert', 'replica')
- codes: bfloat16 [128, 48, 4096], P('expert', 'replica')
- scales: float32 [128, 48, 32], P('expert', 'replica')
- outlier_values: bfloat16 [128, 48, 16], P('expert', 'replica')
Inputs may be any that keep to these rules, and one draw needn't show every extreme that they name: `outlier_channels`: 16 distinct channels for each expert. `destination`: a permutation of the slots; slot s lies on expert index s // 8; of the 8 experts of one expert index, at most 1 go to any one expert index (itself included), and exactly 1 to every index that gets any.
All inputs are finite; a program needn't handle non-finite values.
Results may differ from a plain program's by a relative error of at most 0.002.
Values sent between devices are 32-bit elements; how exact they have to be, the bound alone decides.
No kernel may reach another device: no remote copies, remote signals or barrier semaphores. Data moves between devices by JAX's collectives and lax.ppermute only.
A program may use at most 32 MiB of HBM per device.

v0:
```python
import jax
import jax.numpy as jnp
from jax import lax
from jax.sharding import PartitionSpec as P

GROUP = 128


beta_first = 0.9
beta_second = 0.95
bias_first = 1.0 / (1.0 - 0.9**50)
bias_second = 1.0 / (1.0 - 0.95**50)
epsilon_adam = 1e-08
learn_rate = 0.02
decay_rate = 0.1
quant_epsilon = 1e-06


def adam_update(grad_sum, master, moment, second, loads):
    grad = grad_sum / loads.astype(jnp.float32)[:, None, None]
    moment_next = beta_first * moment + (1.0 - beta_first) * grad
    second_next = beta_second * second + (1.0 - beta_second) * grad * grad
    update = (
        moment_next * bias_first / (jnp.sqrt(second_next * bias_second) + epsilon_adam)
        + decay_rate * master
    )
    return (master - learn_rate * update, moment_next, second_next)


def quantize(weights, channels):
    experts, rows, width = weights.shape
    column = jnp.arange(width, dtype=jnp.int32)
    outlier_mask = jnp.any(channels[:, :, None] == column[None, None, :], axis=1)
    masked = outlier_mask[:, None, :]
    magnitude = jnp.where(masked, 0.0, jnp.abs(weights)).reshape(
        experts, rows, width // GROUP, GROUP
    )
    scale = (jnp.max(magnitude, axis=-1) + quant_epsilon) / 7.0
    ratio = (weights.reshape(experts, rows, width // GROUP, GROUP) / scale[..., None]).reshape(
        experts, rows, width
    )
    codes = jnp.where(masked, 0.0, ratio).astype(jnp.bfloat16)
    picks = channels[:, None, :]
    outliers = jnp.take_along_axis(weights, picks, axis=2).astype(jnp.bfloat16)
    return (codes, scale, outliers)


def route_slots(destination, experts, total, capacity):
    target = destination // experts
    local = destination % experts
    order = jnp.arange(experts, dtype=jnp.int32)
    same = target[:, None] == target[None, :]
    earlier = order[None, :] < order[:, None]
    rank = jnp.sum(jnp.logical_and(same, earlier), axis=1)
    slots = target * capacity + rank
    labels = jnp.full((total,), -1, jnp.int32).at[slots].set(local)
    return (slots, labels)


def packed(array, slots, total):
    return jnp.zeros((total,) + array.shape[1:], array.dtype).at[slots].set(array)


def locate(labels, experts):
    order = jnp.arange(experts, dtype=jnp.int32)
    return jnp.argmax(labels[None, :] == order[:, None], axis=1)


def settle(array, sources):
    return jnp.take(array, sources, axis=0)


def body(gradients, master, moment, second, loads, outlier_channels, destination):
    count = lax.axis_size("expert")
    experts = master.shape[0]
    capacity = max(1, experts // count)
    total = count * capacity
    slots, labels = route_slots(destination, experts, total, capacity)
    terms = gradients[0].astype(jnp.float32)
    grad_sum = lax.psum_scatter(terms, "replica", scatter_dimension=1, tiled=True)
    weights_old, moment_old, second_old = adam_update(grad_sum, master, moment, second, loads)
    moved = (
        lax.all_to_all(
            packed(weights_old, slots, total), "expert", split_axis=0, concat_axis=0, tiled=True
        ),
        lax.all_to_all(
            packed(moment_old, slots, total), "expert", split_axis=0, concat_axis=0, tiled=True
        ),
        lax.all_to_all(
            packed(second_old, slots, total), "expert", split_axis=0, concat_axis=0, tiled=True
        ),
        lax.all_to_all(
            packed(outlier_channels, slots, total),
            "expert",
            split_axis=0,
            concat_axis=0,
            tiled=True,
        ),
        lax.all_to_all(labels, "expert", split_axis=0, concat_axis=0, tiled=True),
    )
    sources = locate(moved[4], experts)
    weights = settle(moved[0], sources)
    moment_next = settle(moved[1], sources)
    second_next = settle(moved[2], sources)
    channels = settle(moved[3], sources)
    codes, scale, outliers = quantize(weights, channels)
    return (weights, moment_next, second_next, codes, scale, outliers)


def solution(mesh):
    in_specs = (
        P("replica", "expert", None, None),
        P("expert", "replica", None),
        P("expert", "replica", None),
        P("expert", "replica", None),
        P("expert"),
        P("expert", None),
        P("expert"),
    )
    out_specs = (
        P("expert", "replica", None),
        P("expert", "replica", None),
        P("expert", "replica", None),
        P("expert", "replica", None),
        P("expert", "replica", None),
        P("expert", "replica", None),
    )
    return jax.shard_map(body, mesh=mesh, in_specs=in_specs, out_specs=out_specs, check_vma=False)
```

profile of v0, /device:TPU:8, one launch (start us, length us, event | category | flops | bytes accessed | tf_op | source)
XLA Modules:
  0.0 288.2 jit_solution(3634691310986950174)
XLA Ops:
  7.2 0.0 reduce-scatter.2.cloned.1.call-start
  7.2 6.4 %bitcast_convert_fusion = f32[8,48,4096]{2,0,1:T(8,128)} fusion(bf16[1,8,48,4096]{3,2,1,0:T(8,128)(2,1)} %param.9), kind=kLoop, calls=%fused_computation.10 | loop fusion | flops 1572864 | bytes 9437184 | tf_op jit(solution)/shard_map/convert_element_type | solution.py:79
  13.6 0.0 copy-start.3
  13.6 0.0 reduce-scatter.2.cloned.1.call-update
  13.6 0.6 copy-done.4
  14.3 0.2 convert_reduce_fusion
  14.4 0.6 scatter_custom_fusion.1
  15.1 0.7 copy.57
  15.7 12.7 %all-to-all-start.1 = ((s32[16,1,1]{2,1,0:T(1,128)}), s32[16,1,1]{2,1,0:T(1,128)S(1)}, u32[]{:S(2)}, u32[]{:S(2)}) async-start(s32[16,1,1]{2,1,0:T(1,128)} %copy.57), calls=%async_computation.2 | async-start | bytes 16384 | tf_op jit(solution)/shard_map/all_to_all | solution.py:99
  28.5 1.3 scatter_custom_fusion.4
  29.8 5.1 %all-to-all-done.1 = s32[16,1,1]{2,1,0:T(1,128)S(1)} async-done(((s32[16,1,1]{2,1,0:T(1,128)}), s32[16,1,1]{2,1,0:T(1,128)S(1)}, u32[]{:S(2)}, u32[]{:S(2)}) %all-to-all-start.1) | async-done | bytes 96 | tf_op jit(solution)/shard_map/all_to_all | solution.py:99
  34.9 4.8 %all-to-all-start.4 = ((s32[16,1,16]{2,1,0:T(1,128)}), s32[16,1,16]{2,1,0:T(1,128)S(1)}, u32[]{:S(2)}, u32[]{:S(2)}) async-start(s32[16,1,16]{2,1,0:T(1,128)} %bitcast.11), calls=%async_computation.5 | async-start | bytes 16384 | tf_op jit(solution)/shard_map/all_to_all | solution.py:92
  39.7 0.4 reduce.19
  40.1 0.6 iota_reduce_fusion
  40.7 191.3 %reduce-scatter.2.cloned.1.call-done = f32[8,1,4096]{2,0,1:T(8,128)} async-done(((f32[8,48,4096]{2,0,1:T(8,128)}), f32[8,1,4096]{2,0,1:T(8,128)}) %reduce-scatter.2.cloned.1.call-update) | async-done | bytes 131088 | tf_op jit(solution)/shard_map/reduce_scatter | solution.py:80
  232.0 1.4 scatter_custom_fusion
  233.4 1.0 reshape.278
  234.4 6.3 %all-to-all-start = ((f32[16,1,4096]{2,1,0:T(1,128)}), f32[16,1,4096]{2,1,0:T(1,128)S(1)}, u32[]{:S(2)}, u32[]{:S(2)}) async-start(f32[16,1,4096]{2,1,0:T(1,128)} %reshape.278), calls=%async_computation.1 | async-start | bytes 524288 | tf_op jit(solution)/shard_map/all_to_all | solution.py:83
  240.8 0.6 gather_fusion
  241.3 0.1 broadcast_select_fusion
  241.4 0.1 fusion.35
  241.5 1.2 scatter_custom_fusion.2
  242.7 1.0 copy.63
  243.7 5.4 %all-to-all-done = f32[16,1,4096]{2,1,0:T(1,128)S(1)} async-done(((f32[16,1,4096]{2,1,0:T(1,128)}), f32[16,1,4096]{2,1,0:T(1,128)S(1)}, u32[]{:S(2)}, u32[]{:S(2)}) %all-to-all-start) | async-done | bytes 262176 | tf_op jit(solution)/shard_map/all_to_all | solution.py:83
  249.1 6.0 %all-to-all-start.2 = ((f32[16,1,4096]{2,1,0:T(1,128)}), f32[16,1,4096]{2,1,0:T(1,128)S(1)}, u32[]{:S(2)}, u32[]{:S(2)}) async-start(f32[16,1,4096]{2,1,0:T(1,128)} %copy.63), calls=%async_computation.3 | async-start | bytes 524288 | tf_op jit(solution)/shard_map/all_to_all | solution.py:86
  255.1 1.0 fusion
  256.1 0.1 reshape.269
  256.2 0.8 scatter_custom_fusion.3
  257.0 1.0 copy.64
  258.0 0.2 copy.101
  258.2 0.6 gather_fusion.2
  258.8 0.2 bitcast_reduce_fusion
  259.0 6.3 %all-to-all-done.2 = f32[16,1,4096]{2,1,0:T(1,128)S(1)} async-done(((f32[16,1,4096]{2,1,0:T(1,128)}), f32[16,1,4096]{2,1,0:T(1,128)S(1)}, u32[]{:S(2)}, u32[]{:S(2)}) %all-to-all-start.2) | async-done | bytes 262176 | tf_op jit(solution)/shard_map/all_to_all | solution.py:86
  265.3 5.3 %all-to-all-start.3 = ((f32[16,1,4096]{2,1,0:T(1,128)}), f32[16,1,4096]{2,1,0:T(1,128)S(1)}, u32[]{:S(2)}, u32[]{:S(2)}) async-start(f32[16,1,4096]{2,1,0:T(1,128)} %copy.64), calls=%async_computation.4 | async-start | bytes 524288 | tf_op jit(solution)/shard_map/all_to_all | solution.py:89
  270.6 0.7 fusion.3
  271.3 0.8 copy.66
  272.1 1.2 gather_fusion.1
  273.4 0.1 reshape.268
  273.5 0.7 copy.69
  274.1 0.2 copy.100
  274.3 0.6 gather_fusion.3
  274.9 0.7 select_convert_fusion
  275.5 3.4 %all-to-all-done.3 = f32[16,1,4096]{2,1,0:T(1,128)S(1)} async-done(((f32[16,1,4096]{2,1,0:T(1,128)}), f32[16,1,4096]{2,1,0:T(1,128)S(1)}, u32[]{:S(2)}, u32[]{:S(2)}) %all-to-all-start.3) | async-done | bytes 262176 | tf_op jit(solution)/shard_map/all_to_all | solution.py:89
  279.0 0.2 copy.99
  279.1 0.6 gather_fusion.4
  279.7 0.1 bitcast_select_fusion
  279.8 0.8 copy.67
  280.6 0.8 copy.68
  (18 shorter events, 0.1 us)
Async XLA Ops:
  7.2 224.8 %reduce-scatter.2.cloned.1.call-start = ((), (), s32[]{:S(2)}) async-start(), calls=%async_computation.6 | async-start | bytes 6422528 | tf_op jit(solution)/shard_map/reduce_scatter | solution.py:80
  13.6 0.7 copy-start.4
  13.6 14.9 %copy-start.5 = (s32[8]{0:T(128)S(1)}, s32[8]{0:T(128)}, u32[]{:S(2)}) copy-start(s32[8]{0:T(128)} %param.13) | copy-start | bytes 100
  13.6 218.4 %copy-start.1 = (f32[8,1,4096]{2,1,0:T(1,128)S(1)}, f32[8,1,4096]{2,1,0:T(1,128)}, u32[]{:S(2)}) copy-start(f32[8,1,4096]{2,1,0:T(1,128)} %param.11) | copy-start | bytes 393220
  13.6 218.4 %copy-start.2 = (f32[8,1,4096]{2,1,0:T(1,128)S(1)}, f32[8,1,4096]{2,1,0:T(1,128)}, u32[]{:S(2)}) copy-start(f32[8,1,4096]{2,1,0:T(1,128)} %param.12) | copy-start | bytes 393220
  13.6 218.4 %copy-start.3 = (f32[8,1,4096]{2,1,0:T(1,128)S(1)}, f32[8,1,4096]{2,1,0:T(1,128)}, u32[]{:S(2)}) copy-start(f32[8,1,4096]{2,1,0:T(1,128)} %param.10) | copy-start | bytes 393220
  15.7 19.2 %all-to-all-start.1 = ((s32[16,1,1]{2,1,0:T(1,128)}), s32[16,1,1]{2,1,0:T(1,128)S(1)}, u32[]{:S(2)}, u32[]{:S(2)}) async-start(s32[16,1,1]{2,1,0:T(1,128)} %copy.57), calls=%async_computation.2 | async-start | bytes 16384 | tf_op jit(solution)/shard_map/all_to_all | solution.py:99
  34.9 199.5 %all-to-all-start.4 = ((s32[16,1,16]{2,1,0:T(1,128)}), s32[16,1,16]{2,1,0:T(1,128)S(1)}, u32[]{:S(2)}, u32[]{:S(2)}) async-start(s32[16,1,16]{2,1,0:T(1,128)} %bitcast.11), calls=%async_computation.5 | async-start | bytes 16384 | tf_op jit(solution)/shard_map/all_to_all | solution.py:92
  232.0 24.2 %copy-start = (f32[8,1,4096]{2,0,1:T(8,128)S(1)}, f32[8,1,4096]{2,0,1:T(8,128)}, u32[]{:S(2)}) copy-start(f32[8,1,4096]{2,0,1:T(8,128)} %reduce-scatter.2.cloned.1.call-done) | copy-start | bytes 393220
  234.4 14.7 %all-to-all-start = ((f32[16,1,4096]{2,1,0:T(1,128)}), f32[16,1,4096]{2,1,0:T(1,128)S(1)}, u32[]{:S(2)}, u32[]{:S(2)}) async-start(f32[16,1,4096]{2,1,0:T(1,128)} %reshape.278), calls=%async_computation.1 | async-start | bytes 524288 | tf_op jit(solution)/shard_map/all_to_all | solution.py:83
  249.1 16.2 %all-to-all-start.2 = ((f32[16,1,4096]{2,1,0:T(1,128)}), f32[16,1,4096]{2,1,0:T(1,128)S(1)}, u32[]{:S(2)}, u32[]{:S(2)}) async-start(f32[16,1,4096]{2,1,0:T(1,128)} %copy.63), calls=%async_computation.3 | async-start | bytes 524288 | tf_op jit(solution)/shard_map/all_to_all | solution.py:86
  265.3 13.7 %all-to-all-start.3 = ((f32[16,1,4096]{2,1,0:T(1,128)}), f32[16,1,4096]{2,1,0:T(1,128)S(1)}, u32[]{:S(2)}, u32[]{:S(2)}) async-start(f32[16,1,4096]{2,1,0:T(1,128)} %copy.64), calls=%async_computation.4 | async-start | bytes 524288 | tf_op jit(solution)/shard_map/all_to_all | solution.py:89
Sparse Core Ops, SparseCore 0:
  13.8 218.2 reduce-scatter.1
where the time goes:
time: 289 us; the launch traced here: 288 us
  waiting for transfers between devices  212 us (73%)
  starting transfers between devices  35.2 us (12%)
  between operations  14.2 us (5%)
  other arithmetic  13.9 us (5%)
  local copies, waits for them, and re-layouts  13.4 us (5%)
    reduce_scatter x1, waiting for transfers between devices, body(): lax.psum_scatter(terms, 'replica', scatter_dimension=1, tiled=True)  191 us
    all_to_all x1, starting transfers between devices, body(): lax.all_to_all(labels, 'expert', split_axis=0, concat_axis=0, tiled=True)  12.7 us
    convert_element_type x1, other arithmetic, body(): terms = gradients[0].astype(jnp.float32)  6.37 us
    all_to_all x1, starting transfers between devices, body(): lax.all_to_all(packed(weights_old, slots, total), 'expert', split_axis=0,...  6.34 us
    all_to_all x1, waiting for transfers between devices, body(): lax.all_to_all(packed(moment_old, slots, total), 'expert', split_axis=0,...  6.33 us
    all_to_all x1, starting transfers between devices, body(): lax.all_to_all(packed(moment_old, slots, total), 'expert', split_axis=0,...  6.03 us
  transfers between devices with their start and end apart: 6, of which 5 were waited for; matrix products, arithmetic and copies ran while one was open for 6% of the time, Pallas kernels for 0%

commit v1 on v0

v1 whole, which is shorter than its diff:
```python
import jax
import jax.numpy as jnp
from jax import lax
from jax.experimental import pallas as pl
from jax.experimental.pallas import tpu as pltpu
from jax.sharding import Mesh
from jax.sharding import PartitionSpec as P

GROUP = 128
beta_first = 0.9
beta_second = 0.95
bias_first = 1.0 / (1.0 - 0.9**50)
bias_second = 1.0 / (1.0 - 0.95**50)
epsilon_adam = 1e-08
learn_rate = 0.02
decay_rate = 0.1
quant_epsilon = 1e-06

F32 = jnp.float32
VM = pltpu.VMEM
SM = pltpu.SMEM
Z = ("m", "s", "c")
E = 8
ROWS = 48
TILES = 32
CHUNK = 8
META = 8
STATE = 3 * TILES + META


def split_kernel(where_ref, g_ref, keep_ref, first_ref, rest_ref, rows_ref):
    core = where_ref[0]
    step = where_ref[1]
    for e in range(E):
        x = g_ref[0, e].astype(F32)
        for r in range(0, ROWS, 8):
            block = jnp.stack([x[r : r + 8, j * 128 : (j + 1) * 128] for j in range(CHUNK)])
            rows_ref[r : r + 8, e] = jnp.swapaxes(block, 0, 1)
    plus = lax.rem(step + 1, 3)
    minus = lax.rem(step + 2, 3)
    ahead = jnp.where(core == 0, plus, minus)
    behind = jnp.where(core == 0, minus, plus)
    other = 1 - core
    for i in range(8):
        keep_ref[0, i] = rows_ref[6 * i + 2 * ahead + core]
        keep_ref[1, i] = rows_ref[6 * i + 2 * behind + core]
        keep_ref[2, i] = rows_ref[6 * i + 2 * step + core]
        first_ref[i] = rows_ref[6 * i + 2 * behind + other]
        rest_ref[0, i] = rows_ref[6 * i + 2 * ahead + other]
        rest_ref[1, i] = rows_ref[6 * i + 2 * step + other]


def split(gradients, where):
    steps = TILES // CHUNK
    return pl.pallas_call(
        split_kernel,
        grid=(steps,),
        in_specs=[
            pl.BlockSpec(memory_space=SM),
            pl.BlockSpec((1, E, ROWS, CHUNK * 128), lambda j: (0, 0, 0, j)),
        ],
        out_specs=[
            pl.BlockSpec((3, 8, E, CHUNK, 128), lambda j: (0, 0, 0, j, 0)),
            pl.BlockSpec((8, E, CHUNK, 128), lambda j: (0, 0, j, 0)),
            pl.BlockSpec((2, 8, E, CHUNK, 128), lambda j: (0, 0, 0, j, 0)),
        ],
        out_shape=[
            jax.ShapeDtypeStruct((3, 8, E, TILES, 128), F32),
            jax.ShapeDtypeStruct((8, E, TILES, 128), F32),
            jax.ShapeDtypeStruct((2, 8, E, TILES, 128), F32),
        ],
        scratch_shapes=[VM((ROWS, E, CHUNK, 128), F32)],
        compiler_params=pltpu.CompilerParams(vmem_limit_bytes=32 << 20),
        name="split_rows",
    )(where, gradients)


def pack_state_kernel(dest_ref, master_ref, moment_ref, second_ref, meta_ref, out_ref):
    out_ref[...] = jnp.full(out_ref.shape, -1.0, F32)
    for e in range(E):
        slot = lax.shift_right_logical(dest_ref[e], 3)
        out_ref[slot, 0:TILES] = master_ref[e]
        out_ref[slot, TILES : 2 * TILES] = moment_ref[e]
        out_ref[slot, 2 * TILES : 3 * TILES] = second_ref[e]
        out_ref[slot, 3 * TILES : STATE] = jnp.broadcast_to(meta_ref[e : e + 1], (META, 128))


def pack_state(destination, master, moment, second, meta):
    return pl.pallas_call(
        pack_state_kernel,
        in_specs=[pl.BlockSpec(memory_space=SM)] + [pl.BlockSpec(memory_space=VM)] * 4,
        out_specs=pl.BlockSpec(memory_space=VM),
        out_shape=jax.ShapeDtypeStruct((16, STATE, 128), F32),
        name="pack_state",
    )(destination, master, moment, second, meta)


def pack_sum_kernel(dest_ref, parts_ref, out_ref):
    out_ref[...] = jnp.zeros(out_ref.shape, F32)
    for e in range(E):
        total = parts_ref[0, e]
        for i in range(1, 8):
            total = total + parts_ref[i, e]
        out_ref[lax.shift_right_logical(dest_ref[e], 3)] = total


def pack_sum(destination, parts):
    return pl.pallas_call(
        pack_sum_kernel,
        in_specs=[pl.BlockSpec(memory_space=SM), pl.BlockSpec(memory_space=VM)],
        out_specs=pl.BlockSpec(memory_space=VM),
        out_shape=jax.ShapeDtypeStruct((16, TILES, 128), F32),
        name="pack_sum",
    )(destination, parts)


def finish_kernel(
    src_ref, loads_ref, chan_ref, grad_ref, state_ref,
    master_ref, moment_ref, second_ref, codes_ref, scale_ref, outlier_ref,
):
    new = []
    for e in range(E):
        src = src_ref[e]
        grad = grad_ref[src] / loads_ref[e]
        master = state_ref[src, 0:TILES]
        moment = beta_first * state_ref[src, TILES : 2 * TILES] + (1.0 - beta_first) * grad
        second = (
            beta_second * state_ref[src, 2 * TILES : 3 * TILES]
            + (1.0 - beta_second) * grad * grad
        )
        update = (
            moment * bias_first / (jnp.sqrt(second * bias_second) + epsilon_adam)
            + decay_rate * master
        )
        weights = master - learn_rate * update
        master_ref[e] = weights
        moment_ref[e] = moment
        second_ref[e] = second
        new.append(weights)
    turned = jnp.swapaxes(jnp.stack(new), 0, 1)
    lane = lax.broadcasted_iota(jnp.int32, (E, 128), 1)
    channels = [jnp.broadcast_to(chan_ref[:, k : k + 1], (E, 128)) for k in range(16)]
    picked = [jnp.zeros((E, 128), F32) for _ in range(16)]
    scales = jnp.zeros((E, 128), F32)
    for g in range(TILES):
        row = turned[g]
        column = lane + g * 128
        masked = jnp.zeros((E, 128), jnp.bool_)
        for k in range(16):
            hit = column == channels[k]
            masked = jnp.logical_or(masked, hit)
            picked[k] = jnp.where(hit, row, picked[k])
        top = jnp.max(jnp.where(masked, 0.0, jnp.abs(row)), axis=1, keepdims=True)
        scale = (top + quant_epsilon) / 7.0
        codes_ref[:, g * 128 : (g + 1) * 128] = jnp.where(masked, 0.0, row / scale).astype(
            jnp.bfloat16
        )
        scales = jnp.where(lane == g, jnp.broadcast_to(scale, (E, 128)), scales)
    scale_ref[...] = scales[:, 0:TILES]
    outliers = jnp.zeros((E, 128), F32)
    for k in range(16):
        value = jnp.sum(picked[k], axis=1, keepdims=True)
        outliers = jnp.where(lane == k, jnp.broadcast_to(value, (E, 128)), outliers)
    outlier_ref[...] = outliers[:, 0:16].astype(jnp.bfloat16)


def finish(sources, loads, channels, grad, state):
    big = jax.ShapeDtypeStruct((E, TILES, 128), F32)
    return pl.pallas_call(
        finish_kernel,
        in_specs=[pl.BlockSpec(memory_space=SM)] * 2 + [pl.BlockSpec(memory_space=VM)] * 3,
        out_specs=[pl.BlockSpec(memory_space=VM)] * 6,
        out_shape=[
            big,
            big,
            big,
            jax.ShapeDtypeStruct((E, TILES * 128), jnp.bfloat16),
            jax.ShapeDtypeStruct((E, TILES), F32),
            jax.ShapeDtypeStruct((E, 16), jnp.bfloat16),
        ],
        name="adam_quantize",
    )(sources, loads, channels, grad, state)


def both_ways(array, turn):
    pairs = []
    for z in range(12):
        pairs.append((2 * z, 2 * ((z + turn) % 12)))
        pairs.append((2 * z + 1, 2 * ((z - turn) % 12) + 1))
    return lax.ppermute(array, Z, pairs)


def body(gradients, master, moment, second, loads, outlier_channels, destination):
    where = jnp.stack([lax.axis_index("c"), lax.axis_index("s")]).astype(jnp.int32)
    keep, first, rest = split(gradients, where)
    swap = [(0, 1), (1, 0)]
    first = keep[0] + lax.ppermute(first, "c", swap)
    rest = lax.ppermute(rest, "c", swap)
    from_first = both_ways(first, 1)
    from_second = both_ways(keep[1] + rest[0], -1)

    meta = jnp.concatenate(
        [jnp.bitwise_and(destination, 7)[:, None], loads[:, None], outlier_channels], axis=1
    ).astype(F32)
    meta = jnp.pad(meta, ((0, 0), (0, 128 - 18)))
    shape = (E, TILES, 128)
    state = pack_state(
        destination, master.reshape(shape), moment.reshape(shape), second.reshape(shape), meta
    )
    state = lax.all_to_all(state, ("x", "y"), split_axis=0, concat_axis=0, tiled=True)
    labels = state[:, 3 * TILES, :18]
    order = jnp.arange(E, dtype=F32)
    sources = jnp.argmax(labels[:, 0][None, :] == order[:, None], axis=1).astype(jnp.int32)
    chosen = jnp.sum(
        jnp.where((labels[:, 0][None, :] == order[:, None])[:, :, None], labels[None], 0.0), axis=1
    )
    loads_here = chosen[:, 1]
    channels_here = chosen[:, 2:18].astype(jnp.int32)

    total = keep[2] + rest[1] + from_first + from_second
    parts = lax.all_to_all(total, ("h", "m"), split_axis=0, concat_axis=0, tiled=True)
    grad = pack_sum(destination, parts)
    grad = lax.all_to_all(grad, ("x", "y"), split_axis=0, concat_axis=0, tiled=True)
    w, m, v, codes, scales, outliers = finish(sources, loads_here, channels_here, grad, state)
    full = (E, 1, TILES * 128)
    return (
        w.reshape(full),
        m.reshape(full),
        v.reshape(full),
        codes[:, None, :],
        scales[:, None, :],
        outliers[:, None, :],
    )


def solution(mesh):
    fine = Mesh(mesh.devices.reshape(4, 4, 2, 4, 3, 2), ("x", "y", "h", "m", "s", "c"))
    expert = ("x", "y")
    replica = ("h", "m", "s", "c")
    state = P(expert, replica, None)
    in_specs = (
        P(replica, expert, None, None),
        state,
        state,
        state,
        P(expert),
        P(expert, None),
        P(expert),
    )
    return jax.shard_map(body, mesh=fine, in_specs=in_specs, out_specs=(state,) * 6, check_vma=False)
```

time: 289 us -> 142 us (0.49)
  the two profiles are of different devices: /device:TPU:8 before, /device:TPU:64 now
where the time goes in v1:
time: 142 us; the launch traced here: 141 us
  waiting for transfers between devices  75.1 us (53%)
  starting transfers between devices  41.1 us (29%)
  Pallas kernels  10.8 us (8%)
  other arithmetic  7.28 us (5%)
  local copies, waits for them, and re-layouts  5.97 us (4%)
    all_to_all x1, waiting for transfers between devices, body(): lax.all_to_all(total, ('h', 'm'), split_axis=0, concat_axis=0, tiled=True)  47.2 us
    ppermute x2, waiting for transfers between devices, both_ways(): return lax.ppermute(array, Z, pairs)  19.1 us
    all_to_all x1, starting transfers between devices, body(): lax.all_to_all(total, ('h', 'm'), split_axis=0, concat_axis=0, tiled=True)  14.1 us
    ppermute x2, starting transfers between devices, both_ways(): return lax.ppermute(array, Z, pairs)  9.3 us
    all_to_all x1, waiting for transfers between devices, body(): lax.all_to_all(grad, ('x', 'y'), split_axis=0, concat_axis=0, tiled=True)  8.81 us
    all_to_all x1, starting transfers between devices, body(): lax.all_to_all(state, ('x', 'y'), split_axis=0, concat_axis=0, tiled=True)  7.49 us
    all_to_all x1, starting transfers between devices, body(): lax.all_to_all(grad, ('x', 'y'), split_axis=0, concat_axis=0, tiled=True)  5.9 us
    pallas_call x1, Pallas kernels, split(): pl.pallas_call(split_kernel, grid=(steps,), in_specs=[pl.BlockSpec(memory...  4.2 us
  transfers between devices with their start and end apart: 7, of which 4 were waited for; matrix products, arithmetic and copies ran while one was open for 7% of the time, Pallas kernels for 1%

profile of v1, /device:TPU:64, one launch (start us, length us, event | category | flops | bytes accessed | tf_op | source)
XLA Modules:
  0.0 141.0 jit_solution(2392887301202867136)
XLA Ops:
  0.6 0.0 copy-start.4
  0.6 0.0 copy-start.5
  0.7 0.0 copy-start.3
  0.7 0.1 pad_add_fusion.where_ref
  0.7 0.0 copy-start
  0.8 1.9 %copy-done = bf16[1,8,48,4096]{3,2,1,0:T(8,128)(2,1)S(1)} copy-done((bf16[1,8,48,4096]{3,2,1,0:T(8,128)(2,1)S(1)}, bf16[1,8,48,4096]{3,2,1,0:T(8,128)(2,1)}, u32[]{:S(2)}) %copy-start) | copy-done | bytes 3145752
  2.6 4.2 %split_rows.1 = (f32[3,8,8,32,128]{4,3,2,1,0:T(8,128)S(1)}, f32[8,8,32,128]{3,2,1,0:T(8,128)}, f32[2,8,8,32,128]{4,3,2,1,0:T(8,128)}) custom-call(s32[2]{0:T(128)S(1)} %pad_add_fusion.where_ref, bf16[1,8,48,4096]{3,2,1,0:T(8,128)(2,1)S(1)} %copy-done), custom_call_target="tpu_custom_call" | custom-call | tf_op jit(solution)/shard_map/split_rows/pallas_call | solution.py:55
  6.8 1.9 %collective-permute-start = (f32[2,8,8,32,128]{4,3,2,1,0:T(8,128)}, f32[2,8,8,32,128]{4,3,2,1,0:T(8,128)}, u32[]{:S(2)}, u32[]{:S(2)}) collective-permute-start(f32[2,8,8,32,128]{4,3,2,1,0:T(8,128)} %get-tuple-element.18), channel_id=1, source_target_pairs={{0,1},{1,0},{2,3},{3,2},{4,5},{5,4},{6,7},{7,6},{8,9},{9,8},{10,11... | collective-permute-start | bytes 6291464 | tf_op jit(solution)/shard_map/ppermute | solution.py:198
  8.8 2.4 %collective-permute-start.1 = (f32[8,8,32,128]{3,2,1,0:T(8,128)}, f32[8,8,32,128]{3,2,1,0:T(8,128)}, u32[]{:S(2)}, u32[]{:S(2)}) collective-permute-start(f32[8,8,32,128]{3,2,1,0:T(8,128)} %get-tuple-element.19), channel_id=1, source_target_pairs={{0,1},{1,0},{2,3},{3,2},{4,5},{5,4},{6,7},{7,6},{8,9},{9,8},{10,11... | collective-permute-start | bytes 3145736 | tf_op jit(solution)/shard_map/ppermute | solution.py:197
  11.2 0.0 copy-done.4
  11.2 0.1 copy.25
  11.3 0.0 copy-done.5
  11.3 0.1 copy.26
  11.4 0.0 copy-done.3
  11.4 0.1 add_convert_fusion
  11.4 0.6 pad.4.meta_ref
  12.0 2.0 %pack_state.1 = f32[16,104,128]{2,1,0:T(8,128)} custom-call(s32[8]{0:T(128)} %dest_ref.3, f32[8,32,128]{2,1,0:T(8,128)} %bitcast.27, f32[8,32,128]{2,1,0:T(8,128)} %bitcast.28, f32[8,32,128]{2,1,0:T(8,128)} %bitcast.29, f32[8,128]{1,0:T(8,128)} %pad.4.meta_ref), custom_call_target="tpu_custom_call" | custom-call | tf_op jit(solution)/shard_map/pack_state/pallas_call | solution.py:89
  14.1 7.5 %all-to-all-start = ((f32[16,104,128]{2,1,0:T(8,128)}), f32[16,104,128]{2,1,0:T(8,128)}, u32[]{:S(2)}, u32[]{:S(2)}) async-start(f32[16,104,128]{2,1,0:T(8,128)} %pack_state.1), calls=%async_computation | async-start | bytes 1703936 | tf_op jit(solution)/shard_map/all_to_all | solution.py:210
  21.6 0.0 collective-permute-done.1
  21.6 1.5 %bitcast_add_fusion = f32[8,8,32,128]{3,2,1,0:T(8,128)S(1)} fusion(f32[8,8,32,128]{3,2,1,0:T(8,128)} %collective-permute-done.1, f32[3,8,8,32,128]{4,3,2,1,0:T(8,128)S(1)} %get-tuple-element.17), kind=kLoop, calls=%fused_computation.6 | loop fusion | flops 262144 | bytes 3145728 | tf_op jit(solution)/shard_map/add | solution.py:197
  23.1 4.3 %collective-permute-start.2 = (f32[8,8,32,128]{3,2,1,0:T(8,128)S(1)}, f32[8,8,32,128]{3,2,1,0:T(8,128)S(1)}, u32[]{:S(2)}, u32[]{:S(2)}) collective-permute-start(f32[8,8,32,128]{3,2,1,0:T(8,128)S(1)} %bitcast_add_fusion), channel_id=1, source_target_pairs={{0,2},{1,23},{2,4},{3,1},{4,6},{5,3},{6,8},{7,5},{8,10},{9,7},{10,... | collective-permute-start | bytes 3145736 | tf_op jit(solution)/shard_map/ppermute | solution.py:190
  27.3 0.0 collective-permute-done
  27.4 1.5 %fusion = f32[8,8,32,128]{3,2,1,0:T(8,128)S(1)} fusion(f32[2,8,8,32,128]{4,3,2,1,0:T(8,128)} %collective-permute-done, f32[3,8,8,32,128]{4,3,2,1,0:T(8,128)S(1)} %get-tuple-element.17), kind=kLoop, calls=%fused_computation.1 | loop fusion | flops 262144 | bytes 3145728 | tf_op jit(solution)/shard_map/add | solution.py:200
  28.8 5.0 %collective-permute-start.3 = (f32[8,8,32,128]{3,2,1,0:T(8,128)S(1)}, f32[8,8,32,128]{3,2,1,0:T(8,128)S(1)}, u32[]{:S(2)}, u32[]{:S(2)}) collective-permute-start(f32[8,8,32,128]{3,2,1,0:T(8,128)S(1)} %fusion), channel_id=1, source_target_pairs={{0,22},{1,3},{2,0},{3,5},{4,2},{5,7},{6,4},{7,9},{8,6},{9,11},{10,... | collective-permute-start | bytes 3145736 | tf_op jit(solution)/shard_map/ppermute | solution.py:190
  33.9 11.5 %collective-permute-done.2 = f32[8,8,32,128]{3,2,1,0:T(8,128)S(1)} collective-permute-done((f32[8,8,32,128]{3,2,1,0:T(8,128)S(1)}, f32[8,8,32,128]{3,2,1,0:T(8,128)S(1)}, u32[]{:S(2)}, u32[]{:S(2)}) %collective-permute-start.2) | collective-permute-done | bytes 1048608 | tf_op jit(solution)/shard_map/ppermute | solution.py:190
  45.3 7.7 %collective-permute-done.3 = f32[8,8,32,128]{3,2,1,0:T(8,128)S(1)} collective-permute-done((f32[8,8,32,128]{3,2,1,0:T(8,128)S(1)}, f32[8,8,32,128]{3,2,1,0:T(8,128)S(1)}, u32[]{:S(2)}, u32[]{:S(2)}) %collective-permute-start.3) | collective-permute-done | bytes 1048608 | tf_op jit(solution)/shard_map/ppermute | solution.py:190
  53.0 2.7 %fusion.3 = f32[8,8,32,128]{3,2,1,0:T(8,128)} fusion(f32[8,8,32,128]{3,2,1,0:T(8,128)S(1)} %collective-permute-done.3, f32[8,8,32,128]{3,2,1,0:T(8,128)S(1)} %collective-permute-done.2, f32[2,8,8,32,128]{4,3,2,1,0:T(8,128)} %collective-permute-done, f32[3,8,8,32,128]{4,3,2,1,0:T(8,128)S(1)} %get-tuple-element.17), kind=kLoop, calls=%fused_computation.5 | loop fusion | flops 786432 | bytes 5242880 | tf_op jit(solution)/shard_map/add | solution.py:220
  55.7 0.0 all-to-all-done.state_ref
  55.7 14.1 %all-to-all-start.1 = ((f32[8,8,32,128]{3,2,1,0:T(8,128)}), f32[8,8,32,128]{3,2,1,0:T(8,128)S(1)}, u32[]{:S(2)}, u32[]{:S(2)}) async-start(f32[8,8,32,128]{3,2,1,0:T(8,128)} %fusion.3), calls=%async_computation.1 | async-start | bytes 2097152 | tf_op jit(solution)/shard_map/all_to_all | solution.py:221
  69.8 0.8 slice.37
  70.7 0.1 slice_reduce_fusion
  70.8 0.1 select_reduce_fusion
  70.9 47.2 %all-to-all-done.1.parts_ref = f32[8,8,32,128]{3,2,1,0:T(8,128)S(1)} async-done(((f32[8,8,32,128]{3,2,1,0:T(8,128)}), f32[8,8,32,128]{3,2,1,0:T(8,128)S(1)}, u32[]{:S(2)}, u32[]{:S(2)}) %all-to-all-start.1) | async-done | bytes 1048608 | tf_op jit(solution)/shard_map/all_to_all | solution.py:221
  118.1 0.0 copy-start.1
  118.1 1.0 copy-done.1
  119.0 2.0 %pack_sum.1 = f32[16,32,128]{2,1,0:T(8,128)} custom-call(s32[8]{0:T(128)} %dest_ref.3, f32[8,8,32,128]{3,2,1,0:T(8,128)} %copy-done.1), custom_call_target="tpu_custom_call" | custom-call | tf_op jit(solution)/shard_map/pack_sum/pallas_call | solution.py:108
  121.1 5.9 %all-to-all-start.2 = ((f32[16,32,128]{2,1,0:T(8,128)}), f32[16,32,128]{2,1,0:T(8,128)S(1)}, u32[]{:S(2)}, u32[]{:S(2)}) async-start(f32[16,32,128]{2,1,0:T(8,128)} %pack_sum.1), calls=%async_computation.2 | async-start | bytes 524288 | tf_op jit(solution)/shard_map/all_to_all | solution.py:223
  127.0 0.7 slice_reduce_fusion.1.loads_ref
  127.6 0.7 iota_reduce_fusion
  128.3 0.7 slice_convert_fusion.chan_ref
  129.0 8.8 %all-to-all-done.2.grad_ref = f32[16,32,128]{2,1,0:T(8,128)S(1)} async-done(((f32[16,32,128]{2,1,0:T(8,128)}), f32[16,32,128]{2,1,0:T(8,128)S(1)}, u32[]{:S(2)}, u32[]{:S(2)}) %all-to-all-start.2) | async-done | bytes 262176 | tf_op jit(solution)/shard_map/all_to_all | solution.py:223
  137.8 0.0 copy-start.2
  137.8 0.7 copy-done.2
  138.5 2.6 %adam_quantize.1 = (f32[8,32,128]{2,1,0:T(8,128)}, f32[8,32,128]{2,1,0:T(8,128)}, f32[8,32,128]{2,1,0:T(8,128)}, bf16[8,4096]{1,0:T(8,128)(2,1)}, f32[8,32]{1,0:T(8,128)}, /*index=5*/bf16[8,16]{1,0:T(8,128)(2,1)}) custom-call(s32[8]{0:T(128)} %get-tuple-element.16.src_ref, f32[8]{0:T(128)} %slice_reduce_fusion.1.loads_ref, ...), custom_call_target="tpu_custom_call" | custom-call | tf_op jit(solution)/shard_map/adam_quantize/pallas_call | solution.py:169
  (2 shorter events, 0.0 us)
Async XLA Ops:
  0.6 10.5 %copy-start.4 = (s32[8]{0:T(128)S(1)}, s32[8]{0:T(128)}, u32[]{:S(2)}) copy-start(s32[8]{0:T(128)} %dest_ref.3) | copy-start | bytes 100
  0.6 10.6 %copy-start.5 = (s32[8]{0:T(128)S(1)}, s32[8]{0:T(128)}, u32[]{:S(2)}) copy-start(s32[8]{0:T(128)} %param.11) | copy-start | bytes 100
  0.7 10.7 %copy-start.3 = (s32[8,16]{1,0:T(8,128)S(1)}, s32[8,16]{1,0:T(8,128)}, u32[]{:S(2)}) copy-start(s32[8,16]{1,0:T(8,128)} %param.12) | copy-start | bytes 1540
  0.7 1.9 %copy-start = (bf16[1,8,48,4096]{3,2,1,0:T(8,128)(2,1)S(1)}, bf16[1,8,48,4096]{3,2,1,0:T(8,128)(2,1)}, u32[]{:S(2)}) copy-start(bf16[1,8,48,4096]{3,2,1,0:T(8,128)(2,1)} %g_ref.1) | copy-start | bytes 9437188
  6.8 20.5 %collective-permute-start = (f32[2,8,8,32,128]{4,3,2,1,0:T(8,128)}, f32[2,8,8,32,128]{4,3,2,1,0:T(8,128)}, u32[]{:S(2)}, u32[]{:S(2)}) collective-permute-start(f32[2,8,8,32,128]{4,3,2,1,0:T(8,128)} %get-tuple-element.18), channel_id=1, source_target_pairs={{0,1},{1,0},{2,3},{3,2},{4,5},{5,4},{6,7},{7,6},{8,9},{9,8},{10,11... | collective-permute-start | bytes 6291464 | tf_op jit(solution)/shard_map/ppermute | solution.py:198
  8.8 12.8 %collective-permute-start.1 = (f32[8,8,32,128]{3,2,1,0:T(8,128)}, f32[8,8,32,128]{3,2,1,0:T(8,128)}, u32[]{:S(2)}, u32[]{:S(2)}) collective-permute-start(f32[8,8,32,128]{3,2,1,0:T(8,128)} %get-tuple-element.19), channel_id=1, source_target_pairs={{0,1},{1,0},{2,3},{3,2},{4,5},{5,4},{6,7},{7,6},{8,9},{9,8},{10,11... | collective-permute-start | bytes 3145736 | tf_op jit(solution)/shard_map/ppermute | solution.py:197
  14.1 41.7 %all-to-all-start = ((f32[16,104,128]{2,1,0:T(8,128)}), f32[16,104,128]{2,1,0:T(8,128)}, u32[]{:S(2)}, u32[]{:S(2)}) async-start(f32[16,104,128]{2,1,0:T(8,128)} %pack_state.1), calls=%async_computation | async-start | bytes 1703936 | tf_op jit(solution)/shard_map/all_to_all | solution.py:210
  23.1 22.3 %collective-permute-start.2 = (f32[8,8,32,128]{3,2,1,0:T(8,128)S(1)}, f32[8,8,32,128]{3,2,1,0:T(8,128)S(1)}, u32[]{:S(2)}, u32[]{:S(2)}) collective-permute-start(f32[8,8,32,128]{3,2,1,0:T(8,128)S(1)} %bitcast_add_fusion), channel_id=1, source_target_pairs={{0,2},{1,23},{2,4},{3,1},{4,6},{5,3},{6,8},{7,5},{8,10},{9,7},{10,... | collective-permute-start | bytes 3145736 | tf_op jit(solution)/shard_map/ppermute | solution.py:190
  28.8 24.2 %collective-permute-start.3 = (f32[8,8,32,128]{3,2,1,0:T(8,128)S(1)}, f32[8,8,32,128]{3,2,1,0:T(8,128)S(1)}, u32[]{:S(2)}, u32[]{:S(2)}) collective-permute-start(f32[8,8,32,128]{3,2,1,0:T(8,128)S(1)} %fusion), channel_id=1, source_target_pairs={{0,22},{1,3},{2,0},{3,5},{4,2},{5,7},{6,4},{7,9},{8,6},{9,11},{10,... | collective-permute-start | bytes 3145736 | tf_op jit(solution)/shard_map/ppermute | solution.py:190
  55.7 62.3 %all-to-all-start.1 = ((f32[8,8,32,128]{3,2,1,0:T(8,128)}), f32[8,8,32,128]{3,2,1,0:T(8,128)S(1)}, u32[]{:S(2)}, u32[]{:S(2)}) async-start(f32[8,8,32,128]{3,2,1,0:T(8,128)} %fusion.3), calls=%async_computation.1 | async-start | bytes 2097152 | tf_op jit(solution)/shard_map/all_to_all | solution.py:221
  118.1 1.0 copy-start.1
  121.1 16.7 %all-to-all-start.2 = ((f32[16,32,128]{2,1,0:T(8,128)}), f32[16,32,128]{2,1,0:T(8,128)S(1)}, u32[]{:S(2)}, u32[]{:S(2)}) async-start(f32[16,32,128]{2,1,0:T(8,128)} %pack_sum.1), calls=%async_computation.2 | async-start | bytes 524288 | tf_op jit(solution)/shard_map/all_to_all | solution.py:223
  137.8 0.7 copy-start.2

commit v2 on v1

--- a/solution.py
+++ b/solution.py
@@ -28,7 +28,9 @@
 STATE = 3 * TILES + META
 
 
-def split_kernel(where_ref, g_ref, keep_ref, first_ref, rest_ref, rows_ref):
+def split_kernel(
+    where_ref, g_ref, ahead_ref, behind_ref, mine_ref, first_ref, rest_ref, rows_ref
+):
     core = where_ref[0]
     step = where_ref[1]
     for e in range(E):
@@ -42,9 +44,9 @@
     behind = jnp.where(core == 0, minus, plus)
     other = 1 - core
     for i in range(8):
-        keep_ref[0, i] = rows_ref[6 * i + 2 * ahead + core]
-        keep_ref[1, i] = rows_ref[6 * i + 2 * behind + core]
-        keep_ref[2, i] = rows_ref[6 * i + 2 * step + core]
+        ahead_ref[i] = rows_ref[6 * i + 2 * ahead + core]
+        behind_ref[i] = rows_ref[6 * i + 2 * behind + core]
+        mine_ref[i] = rows_ref[6 * i + 2 * step + core]
         first_ref[i] = rows_ref[6 * i + 2 * behind + other]
         rest_ref[0, i] = rows_ref[6 * i + 2 * ahead + other]
         rest_ref[1, i] = rows_ref[6 * i + 2 * step + other]
@@ -60,17 +62,21 @@
             pl.BlockSpec((1, E, ROWS, CHUNK * 128), lambda j: (0, 0, 0, j)),
         ],
         out_specs=[
-            pl.BlockSpec((3, 8, E, CHUNK, 128), lambda j: (0, 0, 0, j, 0)),
+            pl.BlockSpec((8, E, CHUNK, 128), lambda j: (0, 0, j, 0)),
+            pl.BlockSpec((8, E, CHUNK, 128), lambda j: (0, 0, j, 0)),
+            pl.BlockSpec((8, E, CHUNK, 128), lambda j: (0, 0, j, 0)),
             pl.BlockSpec((8, E, CHUNK, 128), lambda j: (0, 0, j, 0)),
             pl.BlockSpec((2, 8, E, CHUNK, 128), lambda j: (0, 0, 0, j, 0)),
         ],
         out_shape=[
-            jax.ShapeDtypeStruct((3, 8, E, TILES, 128), F32),
+            jax.ShapeDtypeStruct((8, E, TILES, 128), F32),
+            jax.ShapeDtypeStruct((8, E, TILES, 128), F32),
+            jax.ShapeDtypeStruct((8, E, TILES, 128), F32),
             jax.ShapeDtypeStruct((8, E, TILES, 128), F32),
             jax.ShapeDtypeStruct((2, 8, E, TILES, 128), F32),
         ],
         scratch_shapes=[VM((ROWS, E, CHUNK, 128), F32)],
-        compiler_params=pltpu.CompilerParams(vmem_limit_bytes=32 << 20),
+        compiler_params=pltpu.CompilerParams(vmem_limit_bytes=12 << 20),
         name="split_rows",
     )(where, gradients)
 
@@ -91,6 +97,7 @@
         in_specs=[pl.BlockSpec(memory_space=SM)] + [pl.BlockSpec(memory_space=VM)] * 4,
         out_specs=pl.BlockSpec(memory_space=VM),
         out_shape=jax.ShapeDtypeStruct((16, STATE, 128), F32),
+        compiler_params=pltpu.CompilerParams(vmem_limit_bytes=8 << 20),
         name="pack_state",
     )(destination, master, moment, second, meta)
 
@@ -110,6 +117,7 @@
         in_specs=[pl.BlockSpec(memory_space=SM), pl.BlockSpec(memory_space=VM)],
         out_specs=pl.BlockSpec(memory_space=VM),
         out_shape=jax.ShapeDtypeStruct((16, TILES, 128), F32),
+        compiler_params=pltpu.CompilerParams(vmem_limit_bytes=8 << 20),
         name="pack_sum",
     )(destination, parts)
 
@@ -178,6 +186,7 @@
             jax.ShapeDtypeStruct((E, TILES), F32),
             jax.ShapeDtypeStruct((E, 16), jnp.bfloat16),
         ],
+        compiler_params=pltpu.CompilerParams(vmem_limit_bytes=8 << 20),
         name="adam_quantize",
     )(sources, loads, channels, grad, state)
 
@@ -192,12 +201,12 @@
 
 def body(gradients, master, moment, second, loads, outlier_channels, destination):
     where = jnp.stack([lax.axis_index("c"), lax.axis_index("s")]).astype(jnp.int32)
-    keep, first, rest = split(gradients, where)
+    ahead, behind, mine, first, rest = split(gradients, where)
     swap = [(0, 1), (1, 0)]
-    first = keep[0] + lax.ppermute(first, "c", swap)
+    first = ahead + lax.ppermute(first, "c", swap)
     rest = lax.ppermute(rest, "c", swap)
     from_first = both_ways(first, 1)
-    from_second = both_ways(keep[1] + rest[0], -1)
+    from_second = both_ways(behind + rest[0], -1)
 
     meta = jnp.concatenate(
         [jnp.bitwise_and(destination, 7)[:, None], loads[:, None], outlier_channels], axis=1
@@ -217,7 +226,8 @@
     loads_here = chosen[:, 1]
     channels_here = chosen[:, 2:18].astype(jnp.int32)
 
-    total = keep[2] + rest[1] + from_first + from_second
+    partial = lax.optimization_barrier(mine + rest[1] + from_first)
+    total = partial + from_second
     parts = lax.all_to_all(total, ("h", "m"), split_axis=0, concat_axis=0, tiled=True)
     grad = pack_sum(destination, parts)
     grad = lax.all_to_all(grad, ("x", "y"), split_axis=0, concat_axis=0, tiled=True)

time: 142 us -> 138 us (0.972)
  waiting for transfers between devices: 75.1 us -> 79.3 us
  local copies, waits for them, and re-layouts: 5.97 us -> 2.39 us
  Pallas kernels: 10.8 us -> 8.84 us
    ppermute x2, waiting for transfers between devices: 19.1 us -> 22.4 us  [both_ways(): return lax.ppermute(array, Z, pairs)]
    all_to_all x1, starting transfers between devices: 14.1 us -> 12.2 us  [body(): lax.all_to_all(total, ('h', 'm'), split_axis=0, concat_axis=0, tiled=True)]
    unnamed x12 -> x14, local copies, waits for them, and re-layouts: 3.59 us -> 1.92 us
  transfers between devices with their start and end apart: 7 -> 7, of which waited for: 4 -> 5; matrix products, arithmetic and copies ran while one was open for 7% -> 5% of each run, Pallas kernels for 1% -> 1%
where the time goes in v2:
time: 138 us; the launch traced here: 137 us
  waiting for transfers between devices  79.3 us (57%)
  starting transfers between devices  40.2 us (29%)
  Pallas kernels  8.84 us (6%)
  other arithmetic  5.92 us (4%)
  local copies, waits for them, and re-layouts  2.39 us (2%)
    all_to_all x1, waiting for transfers between devices, body(): lax.all_to_all(total, ('h', 'm'), split_axis=0, concat_axis=0, tiled=True)  47.4 us
    ppermute x2, waiting for transfers between devices, both_ways(): return lax.ppermute(array, Z, pairs)  22.4 us
    all_to_all x1, starting transfers between devices, body(): lax.all_to_all(total, ('h', 'm'), split_axis=0, concat_axis=0, tiled=True)  12.2 us
    ppermute x2, starting transfers between devices, both_ways(): return lax.ppermute(array, Z, pairs)  9.84 us
    all_to_all x1, waiting for transfers between devices, body(): lax.all_to_all(grad, ('x', 'y'), split_axis=0, concat_axis=0, tiled=True)  9.28 us
    all_to_all x1, starting transfers between devices, body(): lax.all_to_all(state, ('x', 'y'), split_axis=0, concat_axis=0, tiled=True)  7.44 us
    all_to_all x1, starting transfers between devices, body(): lax.all_to_all(grad, ('x', 'y'), split_axis=0, concat_axis=0, tiled=True)  6.21 us
    pallas_call x1, Pallas kernels, split(): pl.pallas_call(split_kernel, grid=(steps,), in_specs=[pl.BlockSpec(memory...  4.19 us
  transfers between devices with their start and end apart: 7, of which 5 were waited for; matrix products, arithmetic and copies ran while one was open for 5% of the time, Pallas kernels for 1%

profile of v2, /device:TPU:64, one launch (start us, length us, event | category | flops | bytes accessed | tf_op | source)
XLA Modules:
  0.0 137.4 jit_solution(6546538298419127608)
XLA Ops:
  0.6 0.1 pad_add_fusion.where_ref
  0.7 0.0 copy-start
  0.7 1.9 %copy-done = bf16[1,8,48,4096]{3,2,1,0:T(8,128)(2,1)S(1)} copy-done((bf16[1,8,48,4096]{3,2,1,0:T(8,128)(2,1)S(1)}, bf16[1,8,48,4096]{3,2,1,0:T(8,128)(2,1)}, u32[]{:S(2)}) %copy-start) | copy-done | bytes 3145752
  2.6 4.2 %split_rows.1 = (f32[8,8,32,128]{3,2,1,0:T(8,128)S(1)}, f32[8,8,32,128]{3,2,1,0:T(8,128)S(1)}, f32[8,8,32,128]{3,2,1,0:T(8,128)S(1)}, f32[8,8,32,128]{3,2,1,0:T(8,128)S(1)}, f32[2,8,8,32,128]{4,3,2,1,0:T(8,128)}) custom-call(s32[2]{0:T(128)S(1)} %pad_add_fusion.where_ref, bf16[1,8,48,4096]{3,2,1,0:T(8,128)(2,1)S(1)} %copy-done), custom_call_target="tpu_custom_call" | custom-call | tf_op jit(solution)/shard_map/split_rows/pallas_call | solution.py:57
  6.8 0.0 copy-start.4
  6.8 0.0 copy-start.6
  6.8 0.0 copy-start.5
  6.8 0.0 copy-start.1
  6.8 0.0 copy-start.2
  6.8 0.0 copy-start.3
  6.8 2.1 %collective-permute-start.1 = (f32[8,8,32,128]{3,2,1,0:T(8,128)S(1)}, f32[8,8,32,128]{3,2,1,0:T(8,128)S(1)}, u32[]{:S(2)}, u32[]{:S(2)}) collective-permute-start(f32[8,8,32,128]{3,2,1,0:T(8,128)S(1)} %get-tuple-element.22), channel_id=1, source_target_pairs={{0,1},{1,0},{2,3},{3,2},{4,5},{5,4},{6,7},{7,6},{8,9},{9,8},{10,11... | collective-permute-start | bytes 3145736 | tf_op jit(solution)/shard_map/ppermute | solution.py:206
  8.9 2.4 %collective-permute-start = (f32[2,8,8,32,128]{4,3,2,1,0:T(8,128)}, f32[2,8,8,32,128]{4,3,2,1,0:T(8,128)}, u32[]{:S(2)}, u32[]{:S(2)}) collective-permute-start(f32[2,8,8,32,128]{4,3,2,1,0:T(8,128)} %get-tuple-element.20), channel_id=1, source_target_pairs={{0,1},{1,0},{2,3},{3,2},{4,5},{5,4},{6,7},{7,6},{8,9},{9,8},{10,11... | collective-permute-start | bytes 6291464 | tf_op jit(solution)/shard_map/ppermute | solution.py:207
  11.3 0.2 collective-permute-done.1
  11.5 1.3 add.18
  12.8 4.3 %collective-permute-start.2 = (f32[8,8,32,128]{3,2,1,0:T(8,128)}, f32[8,8,32,128]{3,2,1,0:T(8,128)}, u32[]{:S(2)}, u32[]{:S(2)}) collective-permute-start(f32[8,8,32,128]{3,2,1,0:T(8,128)} %add.18), channel_id=1, source_target_pairs={{0,2},{1,23},{2,4},{3,1},{4,6},{5,3},{6,8},{7,5},{8,10},{9,7},{10,... | collective-permute-start | bytes 3145736 | tf_op jit(solution)/shard_map/ppermute | solution.py:199
  17.1 0.0 copy-done.4
  17.1 0.1 copy.25
  17.2 0.0 copy-done.6
  17.2 0.1 copy.26
  17.3 0.0 copy-done.5
  17.3 0.1 add_convert_fusion
  17.4 0.0 copy-done.1
  17.4 0.0 copy-done.2
  17.4 0.0 copy-done.3
  17.4 1.5 %pack_state.1 = f32[16,104,128]{2,1,0:T(8,128)} custom-call(s32[8]{0:T(128)S(1)} %copy-done.4, f32[8,32,128]{2,1,0:T(8,128)S(1)} %bitcast.27, f32[8,32,128]{2,1,0:T(8,128)S(1)} %bitcast.28, f32[8,32,128]{2,1,0:T(8,128)S(1)} %bitcast.29, f32[8,128]{1,0:T(8,128)S(1)} %pad.4.meta_ref), custom_call_target="tpu_custom_call" | custom-call | tf_op jit(solution)/shard_map/pack_state/pallas_call | solution.py:95
  18.9 7.4 %all-to-all-start = ((f32[16,104,128]{2,1,0:T(8,128)}), f32[16,104,128]{2,1,0:T(8,128)S(1)}, u32[]{:S(2)}, u32[]{:S(2)}) async-start(f32[16,104,128]{2,1,0:T(8,128)} %pack_state.1), calls=%async_computation | async-start | bytes 1703936 | tf_op jit(solution)/shard_map/all_to_all | solution.py:219
  26.3 10.1 %collective-permute-done.2 = f32[8,8,32,128]{3,2,1,0:T(8,128)} collective-permute-done((f32[8,8,32,128]{3,2,1,0:T(8,128)}, f32[8,8,32,128]{3,2,1,0:T(8,128)}, u32[]{:S(2)}, u32[]{:S(2)}) %collective-permute-start.2) | collective-permute-done | bytes 1048608 | tf_op jit(solution)/shard_map/ppermute | solution.py:199
  36.5 0.0 collective-permute-done
  36.5 2.5 %fusion = (f32[8,8,32,128]{3,2,1,0:T(8,128)S(1)}, f32[8,8,32,128]{3,2,1,0:T(8,128)S(1)}) fusion(f32[8,8,32,128]{3,2,1,0:T(8,128)S(1)} %get-tuple-element.23, f32[2,8,8,32,128]{4,3,2,1,0:T(8,128)} %collective-permute-done, f32[8,8,32,128]{3,2,1,0:T(8,128)} %collective-permute-done.2, f32[8,8,32,128]{3,2,1,0:T(8,128)S(1)} %get-tuple-element.19), kind=kLoop, calls=%fused_computation.1 | loop fusion | flops 786432 | bytes 7340032 | tf_op jit(solution)/shard_map/add | solution.py:209
  38.9 5.6 %collective-permute-start.3 = (f32[8,8,32,128]{3,2,1,0:T(8,128)S(1)}, f32[8,8,32,128]{3,2,1,0:T(8,128)S(1)}, u32[]{:S(2)}, u32[]{:S(2)}) collective-permute-start(f32[8,8,32,128]{3,2,1,0:T(8,128)S(1)} %get-tuple-element.48), channel_id=1, source_target_pairs={{0,22},{1,3},{2,0},{3,5},{4,2},{5,7},{6,4},{7,9},{8,6},{9,11},{10,... | collective-permute-start | bytes 3145736 | tf_op jit(solution)/shard_map/ppermute | solution.py:199
  44.5 12.3 %collective-permute-done.3 = f32[8,8,32,128]{3,2,1,0:T(8,128)S(1)} collective-permute-done((f32[8,8,32,128]{3,2,1,0:T(8,128)S(1)}, f32[8,8,32,128]{3,2,1,0:T(8,128)S(1)}, u32[]{:S(2)}, u32[]{:S(2)}) %collective-permute-start.3) | collective-permute-done | bytes 1048608 | tf_op jit(solution)/shard_map/ppermute | solution.py:199
  56.8 1.2 add.21
  58.0 0.0 all-to-all-done.state_ref
  58.0 12.2 %all-to-all-start.1 = ((f32[8,8,32,128]{3,2,1,0:T(8,128)}), f32[8,8,32,128]{3,2,1,0:T(8,128)S(1)}, u32[]{:S(2)}, u32[]{:S(2)}) async-start(f32[8,8,32,128]{3,2,1,0:T(8,128)} %add.21), calls=%async_computation.1 | async-start | bytes 2097152 | tf_op jit(solution)/shard_map/all_to_all | solution.py:231
  70.3 0.1 slice_reduce_fusion
  70.4 0.1 select_reduce_fusion
  70.5 47.4 %all-to-all-done.1.parts_ref = f32[8,8,32,128]{3,2,1,0:T(8,128)S(1)} async-done(((f32[8,8,32,128]{3,2,1,0:T(8,128)}), f32[8,8,32,128]{3,2,1,0:T(8,128)S(1)}, u32[]{:S(2)}, u32[]{:S(2)}) %all-to-all-start.1) | async-done | bytes 1048608 | tf_op jit(solution)/shard_map/all_to_all | solution.py:231
  117.9 1.3 pack_sum.1
  119.2 6.2 %all-to-all-start.2 = ((f32[16,32,128]{2,1,0:T(8,128)}), f32[16,32,128]{2,1,0:T(8,128)S(1)}, u32[]{:S(2)}, u32[]{:S(2)}) async-start(f32[16,32,128]{2,1,0:T(8,128)} %pack_sum.1), calls=%async_computation.2 | async-start | bytes 524288 | tf_op jit(solution)/shard_map/all_to_all | solution.py:233
  125.4 0.2 slice_reduce_fusion.1.loads_ref
  125.6 0.6 iota_reduce_fusion
  126.2 0.1 slice_convert_fusion.chan_ref
  126.3 9.3 %all-to-all-done.2.grad_ref = f32[16,32,128]{2,1,0:T(8,128)S(1)} async-done(((f32[16,32,128]{2,1,0:T(8,128)}), f32[16,32,128]{2,1,0:T(8,128)S(1)}, u32[]{:S(2)}, u32[]{:S(2)}) %all-to-all-start.2) | async-done | bytes 262176 | tf_op jit(solution)/shard_map/all_to_all | solution.py:233
  135.6 1.8 %adam_quantize.1 = (f32[8,32,128]{2,1,0:T(8,128)}, f32[8,32,128]{2,1,0:T(8,128)}, f32[8,32,128]{2,1,0:T(8,128)}, bf16[8,4096]{1,0:T(8,128)(2,1)}, f32[8,32]{1,0:T(8,128)}, /*index=5*/bf16[8,16]{1,0:T(8,128)(2,1)}) custom-call(s32[8]{0:T(128)S(1)} %get-tuple-element.18.src_ref, f32[8]{0:T(128)S(1)} %slice_reduce_fusion.1.loads_ref, ...), custom_call_target="tpu_custom_call" | custom-call | tf_op jit(solution)/shard_map/adam_quantize/pallas_call | solution.py:177
  (4 shorter events, 0.0 us)
Async XLA Ops:
  0.7 1.9 %copy-start = (bf16[1,8,48,4096]{3,2,1,0:T(8,128)(2,1)S(1)}, bf16[1,8,48,4096]{3,2,1,0:T(8,128)(2,1)}, u32[]{:S(2)}) copy-start(bf16[1,8,48,4096]{3,2,1,0:T(8,128)(2,1)} %g_ref.1) | copy-start | bytes 9437188
  6.8 10.3 %copy-start.4 = (s32[8]{0:T(128)S(1)}, s32[8]{0:T(128)}, u32[]{:S(2)}) copy-start(s32[8]{0:T(128)} %dest_ref.3) | copy-start | bytes 100
  6.8 10.4 %copy-start.6 = (s32[8]{0:T(128)S(1)}, s32[8]{0:T(128)}, u32[]{:S(2)}) copy-start(s32[8]{0:T(128)} %param.11) | copy-start | bytes 100
  6.8 10.5 %copy-start.5 = (s32[8,16]{1,0:T(8,128)S(1)}, s32[8,16]{1,0:T(8,128)}, u32[]{:S(2)}) copy-start(s32[8,16]{1,0:T(8,128)} %param.12) | copy-start | bytes 1540
  6.8 10.5 %copy-start.1 = (f32[8,1,4096]{2,1,0:T(1,128)S(1)}, f32[8,1,4096]{2,1,0:T(1,128)}, u32[]{:S(2)}) copy-start(f32[8,1,4096]{2,1,0:T(1,128)} %param.8) | copy-start | bytes 393220
  6.8 10.5 %copy-start.2 = (f32[8,1,4096]{2,1,0:T(1,128)S(1)}, f32[8,1,4096]{2,1,0:T(1,128)}, u32[]{:S(2)}) copy-start(f32[8,1,4096]{2,1,0:T(1,128)} %param.9) | copy-start | bytes 393220
  6.8 10.5 %copy-start.3 = (f32[8,1,4096]{2,1,0:T(1,128)S(1)}, f32[8,1,4096]{2,1,0:T(1,128)}, u32[]{:S(2)}) copy-start(f32[8,1,4096]{2,1,0:T(1,128)} %param.10) | copy-start | bytes 393220
  6.8 4.7 %collective-permute-start.1 = (f32[8,8,32,128]{3,2,1,0:T(8,128)S(1)}, f32[8,8,32,128]{3,2,1,0:T(8,128)S(1)}, u32[]{:S(2)}, u32[]{:S(2)}) collective-permute-start(f32[8,8,32,128]{3,2,1,0:T(8,128)S(1)} %get-tuple-element.22), channel_id=1, source_target_pairs={{0,1},{1,0},{2,3},{3,2},{4,5},{5,4},{6,7},{7,6},{8,9},{9,8},{10,11... | collective-permute-start | bytes 3145736 | tf_op jit(solution)/shard_map/ppermute | solution.py:206
  8.9 27.6 %collective-permute-start = (f32[2,8,8,32,128]{4,3,2,1,0:T(8,128)}, f32[2,8,8,32,128]{4,3,2,1,0:T(8,128)}, u32[]{:S(2)}, u32[]{:S(2)}) collective-permute-start(f32[2,8,8,32,128]{4,3,2,1,0:T(8,128)} %get-tuple-element.20), channel_id=1, source_target_pairs={{0,1},{1,0},{2,3},{3,2},{4,5},{5,4},{6,7},{7,6},{8,9},{9,8},{10,11... | collective-permute-start | bytes 6291464 | tf_op jit(solution)/shard_map/ppermute | solution.py:207
  12.8 23.6 %collective-permute-start.2 = (f32[8,8,32,128]{3,2,1,0:T(8,128)}, f32[8,8,32,128]{3,2,1,0:T(8,128)}, u32[]{:S(2)}, u32[]{:S(2)}) collective-permute-start(f32[8,8,32,128]{3,2,1,0:T(8,128)} %add.18), channel_id=1, source_target_pairs={{0,2},{1,23},{2,4},{3,1},{4,6},{5,3},{6,8},{7,5},{8,10},{9,7},{10,... | collective-permute-start | bytes 3145736 | tf_op jit(solution)/shard_map/ppermute | solution.py:199
  18.9 39.1 %all-to-all-start = ((f32[16,104,128]{2,1,0:T(8,128)}), f32[16,104,128]{2,1,0:T(8,128)S(1)}, u32[]{:S(2)}, u32[]{:S(2)}) async-start(f32[16,104,128]{2,1,0:T(8,128)} %pack_state.1), calls=%async_computation | async-start | bytes 1703936 | tf_op jit(solution)/shard_map/all_to_all | solution.py:219
  38.9 17.9 %collective-permute-start.3 = (f32[8,8,32,128]{3,2,1,0:T(8,128)S(1)}, f32[8,8,32,128]{3,2,1,0:T(8,128)S(1)}, u32[]{:S(2)}, u32[]{:S(2)}) collective-permute-start(f32[8,8,32,128]{3,2,1,0:T(8,128)S(1)} %get-tuple-element.48), channel_id=1, source_target_pairs={{0,22},{1,3},{2,0},{3,5},{4,2},{5,7},{6,4},{7,9},{8,6},{9,11},{10,... | collective-permute-start | bytes 3145736 | tf_op jit(solution)/shard_map/ppermute | solution.py:199
  58.0 59.9 %all-to-all-start.1 = ((f32[8,8,32,128]{3,2,1,0:T(8,128)}), f32[8,8,32,128]{3,2,1,0:T(8,128)S(1)}, u32[]{:S(2)}, u32[]{:S(2)}) async-start(f32[8,8,32,128]{3,2,1,0:T(8,128)} %add.21), calls=%async_computation.1 | async-start | bytes 2097152 | tf_op jit(solution)/shard_map/all_to_all | solution.py:231
  119.2 16.4 %all-to-all-start.2 = ((f32[16,32,128]{2,1,0:T(8,128)}), f32[16,32,128]{2,1,0:T(8,128)S(1)}, u32[]{:S(2)}, u32[]{:S(2)}) async-start(f32[16,32,128]{2,1,0:T(8,128)} %pack_sum.1), calls=%async_computation.2 | async-start | bytes 524288 | tf_op jit(solution)/shard_map/all_to_all | solution.py:233

commit v3 on v2

--- a/solution.py
+++ b/solution.py
@@ -29,7 +29,7 @@
 
 
 def split_kernel(
-    where_ref, g_ref, ahead_ref, behind_ref, mine_ref, first_ref, rest_ref, rows_ref
+    where_ref, g_ref, ahead_ref, behind_ref, mine_ref, first_ref, next_ref, last_ref, rows_ref
 ):
     core = where_ref[0]
     step = where_ref[1]
@@ -48,8 +48,8 @@
         behind_ref[i] = rows_ref[6 * i + 2 * behind + core]
         mine_ref[i] = rows_ref[6 * i + 2 * step + core]
         first_ref[i] = rows_ref[6 * i + 2 * behind + other]
-        rest_ref[0, i] = rows_ref[6 * i + 2 * ahead + other]
-        rest_ref[1, i] = rows_ref[6 * i + 2 * step + other]
+        next_ref[i] = rows_ref[6 * i + 2 * ahead + other]
+        last_ref[i] = rows_ref[6 * i + 2 * step + other]
 
 
 def split(gradients, where):
@@ -61,20 +61,8 @@
             pl.BlockSpec(memory_space=SM),
             pl.BlockSpec((1, E, ROWS, CHUNK * 128), lambda j: (0, 0, 0, j)),
         ],
-        out_specs=[
-            pl.BlockSpec((8, E, CHUNK, 128), lambda j: (0, 0, j, 0)),
-            pl.BlockSpec((8, E, CHUNK, 128), lambda j: (0, 0, j, 0)),
-            pl.BlockSpec((8, E, CHUNK, 128), lambda j: (0, 0, j, 0)),
-            pl.BlockSpec((8, E, CHUNK, 128), lambda j: (0, 0, j, 0)),
-            pl.BlockSpec((2, 8, E, CHUNK, 128), lambda j: (0, 0, 0, j, 0)),
-        ],
-        out_shape=[
-            jax.ShapeDtypeStruct((8, E, TILES, 128), F32),
-            jax.ShapeDtypeStruct((8, E, TILES, 128), F32),
-            jax.ShapeDtypeStruct((8, E, TILES, 128), F32),
-            jax.ShapeDtypeStruct((8, E, TILES, 128), F32),
-            jax.ShapeDtypeStruct((2, 8, E, TILES, 128), F32),
-        ],
+        out_specs=[pl.BlockSpec((8, E, CHUNK, 128), lambda j: (0, 0, j, 0))] * 6,
+        out_shape=[jax.ShapeDtypeStruct((8, E, TILES, 128), F32)] * 6,
         scratch_shapes=[VM((ROWS, E, CHUNK, 128), F32)],
         compiler_params=pltpu.CompilerParams(vmem_limit_bytes=12 << 20),
         name="split_rows",
@@ -201,12 +189,14 @@
 
 def body(gradients, master, moment, second, loads, outlier_channels, destination):
     where = jnp.stack([lax.axis_index("c"), lax.axis_index("s")]).astype(jnp.int32)
-    ahead, behind, mine, first, rest = split(gradients, where)
+    ahead, behind, mine, first, follow, last = split(gradients, where)
     swap = [(0, 1), (1, 0)]
     first = ahead + lax.ppermute(first, "c", swap)
-    rest = lax.ppermute(rest, "c", swap)
+    follow = lax.ppermute(follow, "c", swap)
+    last = lax.ppermute(last, "c", swap)
     from_first = both_ways(first, 1)
-    from_second = both_ways(behind + rest[0], -1)
+    outgoing, from_first = lax.optimization_barrier((behind + follow, from_first))
+    from_second = both_ways(outgoing, -1)
 
     meta = jnp.concatenate(
         [jnp.bitwise_and(destination, 7)[:, None], loads[:, None], outlier_channels], axis=1
@@ -226,7 +216,7 @@
     loads_here = chosen[:, 1]
     channels_here = chosen[:, 2:18].astype(jnp.int32)
 
-    partial = lax.optimization_barrier(mine + rest[1] + from_first)
+    partial = lax.optimization_barrier(mine + last + from_first)
     total = partial + from_second
     parts = lax.all_to_all(total, ("h", "m"), split_axis=0, concat_axis=0, tiled=True)
     grad = pack_sum(destination, parts)

time: 138 us -> 135 us (0.978)
  waiting for transfers between devices: 79.3 us -> 72.4 us
  starting transfers between devices: 40.2 us -> 43.9 us
    ppermute x2, waiting for transfers between devices: 22.4 us -> 15 us  [both_ways(): return lax.ppermute(array, Z, pairs)]
    ppermute x1 -> x2, starting transfers between devices: 2.41 us -> 6.65 us  [the longest x1 4.24 us: body(): last = lax.ppermute(last, 'c', swap)]
    add x1 -> x2, other arithmetic: 2.47 us -> 3.05 us  [the longest x1 1.58 us: body(): partial = lax.optimization_barrier(mine + last + from_first)]
  transfers between devices with their start and end apart: 7 -> 8, of which waited for: 5 -> 5; matrix products, arithmetic and copies ran while one was open for 5% -> 5% of each run, Pallas kernels for 1% -> 1%
where the time goes in v3:
time: 135 us
  waiting for transfers between devices  72.4 us (54%)
  starting transfers between devices  43.9 us (33%)
  Pallas kernels  8.71 us (6%)
  other arithmetic  6.46 us (5%)
  local copies, waits for them, and re-layouts  2.39 us (2%)
    all_to_all x1, waiting for transfers between devices, body(): lax.all_to_all(total, ('h', 'm'), split_axis=0, concat_axis=0, tiled=True)  47.3 us
    ppermute x2, waiting for transfers between devices, both_ways(): return lax.ppermute(array, Z, pairs)  15 us
    all_to_all x1, starting transfers between devices, body(): lax.all_to_all(total, ('h', 'm'), split_axis=0, concat_axis=0, tiled=True)  12.2 us
    ppermute x2, starting transfers between devices, both_ways(): return lax.ppermute(array, Z, pairs)  9.83 us
    all_to_all x1, waiting for transfers between devices, body(): lax.all_to_all(grad, ('x', 'y'), split_axis=0, concat_axis=0, tiled=True)  9.78 us
    all_to_all x1, starting transfers between devices, body(): lax.all_to_all(state, ('x', 'y'), split_axis=0, concat_axis=0, tiled=True)  7.44 us
    all_to_all x1, starting transfers between devices, body(): lax.all_to_all(grad, ('x', 'y'), split_axis=0, concat_axis=0, tiled=True)  5.79 us
    ppermute x1, starting transfers between devices, body(): last = lax.ppermute(last, 'c', swap)  4.24 us
  transfers between devices with their start and end apart: 8, of which 5 were waited for; matrix products, arithmetic and copies ran while one was open for 5% of the time, Pallas kernels for 1%

profile of v3, /device:TPU:64, one launch (start us, length us, event | category | flops | bytes accessed | tf_op | source)
XLA Modules:
  0.0 134.6 jit_solution(2945411311436719372)
XLA Ops:
  0.6 0.1 pad_add_fusion.where_ref
  0.7 0.0 copy-start
  0.7 1.9 %copy-done = bf16[1,8,48,4096]{3,2,1,0:T(8,128)(2,1)S(1)} copy-done((bf16[1,8,48,4096]{3,2,1,0:T(8,128)(2,1)S(1)}, bf16[1,8,48,4096]{3,2,1,0:T(8,128)(2,1)}, u32[]{:S(2)}) %copy-start) | copy-done | bytes 3145752
  2.6 0.0 copy-start.4
  2.6 0.0 copy-start.6
  2.6 0.0 copy-start.1
  2.6 0.0 copy-start.2
  2.6 0.0 copy-start.3
  2.6 4.0 %split_rows.1 = (f32[8,8,32,128]{3,2,1,0:T(8,128)S(1)}, f32[8,8,32,128]{3,2,1,0:T(8,128)S(1)}, f32[8,8,32,128]{3,2,1,0:T(8,128)S(1)}, f32[8,8,32,128]{3,2,1,0:T(...) custom-call(s32[2]{0:T(128)S(1)} %pad_add_fusion.where_ref, bf16[1,8,48,4096]{3,2,1,0:T(8,128)(2,1)S(1)} %copy-done), custom_call_target="tpu_custom_call" | custom-call | tf_op jit(solution)/shard_map/split_rows/pallas_call | solution.py:57
  6.7 0.0 copy-start.5
  6.7 1.9 %collective-permute-start.2 = (f32[8,8,32,128]{3,2,1,0:T(8,128)S(1)}, f32[8,8,32,128]{3,2,1,0:T(8,128)S(1)}, u32[]{:S(2)}, u32[]{:S(2)}) collective-permute-start(f32[8,8,32,128]{3,2,1,0:T(8,128)S(1)} %get-tuple-element.27), channel_id=1, source_target_pairs={{0,1},{1,0},{2,3},{3,2},{4,5},{5,4},{6,7},{7,6},{8,9},{9,8},{10,11... | collective-permute-start | bytes 3145736 | tf_op jit(solution)/shard_map/ppermute | solution.py:194
  8.6 2.4 %collective-permute-start.1 = (f32[8,8,32,128]{3,2,1,0:T(8,128)}, f32[8,8,32,128]{3,2,1,0:T(8,128)}, u32[]{:S(2)}, u32[]{:S(2)}) collective-permute-start(f32[8,8,32,128]{3,2,1,0:T(8,128)} %get-tuple-element.25), channel_id=1, source_target_pairs={{0,1},{1,0},{2,3},{3,2},{4,5},{5,4},{6,7},{7,6},{8,9},{9,8},{10,11... | collective-permute-start | bytes 3145736 | tf_op jit(solution)/shard_map/ppermute | solution.py:195
  11.0 0.2 collective-permute-done.2
  11.2 1.2 add.19
  12.5 0.0 copy-done.5
  12.5 4.3 %collective-permute-start.3 = (f32[8,8,32,128]{3,2,1,0:T(8,128)}, f32[8,8,32,128]{3,2,1,0:T(8,128)}, u32[]{:S(2)}, u32[]{:S(2)}) collective-permute-start(f32[8,8,32,128]{3,2,1,0:T(8,128)} %add.19), channel_id=1, source_target_pairs={{0,2},{1,23},{2,4},{3,1},{4,6},{5,3},{6,8},{7,5},{8,10},{9,7},{10,... | collective-permute-start | bytes 3145736 | tf_op jit(solution)/shard_map/ppermute | solution.py:187
  16.7 0.0 copy-done.4
  16.8 0.1 copy.25
  16.8 0.0 copy-done.7
  16.8 0.1 copy.26
  16.9 0.0 copy-done.6
  16.9 0.1 add_convert_fusion
  17.0 0.0 copy-done.1
  17.0 0.0 copy-done.2
  17.0 0.0 copy-done.3
  17.0 1.6 %pack_state.1 = f32[16,104,128]{2,1,0:T(8,128)} custom-call(s32[8]{0:T(128)S(1)} %copy-done.4, f32[8,32,128]{2,1,0:T(8,128)S(1)} %bitcast.17, f32[8,32,128]{2,1,0:T(8,128)S(1)} %bitcast.18, f32[8,32,128]{2,1,0:T(8,128)S(1)} %bitcast.19, f32[8,128]{1,0:T(8,128)S(1)} %pad.4.meta_ref), custom_call_target="tpu_custom_call" | custom-call | tf_op jit(solution)/shard_map/pack_state/pallas_call | solution.py:83
  18.6 7.4 %all-to-all-start = ((f32[16,104,128]{2,1,0:T(8,128)}), f32[16,104,128]{2,1,0:T(8,128)S(1)}, u32[]{:S(2)}, u32[]{:S(2)}) async-start(f32[16,104,128]{2,1,0:T(8,128)} %pack_state.1), calls=%async_computation | async-start | bytes 1703936 | tf_op jit(solution)/shard_map/all_to_all | solution.py:209
  26.0 4.2 %collective-permute-start = (f32[8,8,32,128]{3,2,1,0:T(8,128)}, f32[8,8,32,128]{3,2,1,0:T(8,128)S(1)}, u32[]{:S(2)}, u32[]{:S(2)}) collective-permute-start(f32[8,8,32,128]{3,2,1,0:T(8,128)} %copy-done.5), channel_id=1, source_target_pairs={{0,1},{1,0},{2,3},{3,2},{4,5},{5,4},{6,7},{7,6},{8,9},{9,8},{10,11... | collective-permute-start | bytes 3145736 | tf_op jit(solution)/shard_map/ppermute | solution.py:196
  30.3 0.0 collective-permute-done.1
  30.3 1.5 %add.18 = f32[8,8,32,128]{3,2,1,0:T(8,128)S(1)} add(f32[8,8,32,128]{3,2,1,0:T(8,128)S(1)} %get-tuple-element.24, f32[8,8,32,128]{3,2,1,0:T(8,128)} %collective-permute-done.1) | non-fusion elementwise | flops 262144 | bytes 3145728 | tf_op jit(solution)/shard_map/add | solution.py:198
  31.8 4.3 %collective-permute-done.3 = f32[8,8,32,128]{3,2,1,0:T(8,128)} collective-permute-done((f32[8,8,32,128]{3,2,1,0:T(8,128)}, f32[8,8,32,128]{3,2,1,0:T(8,128)}, u32[]{:S(2)}, u32[]{:S(2)}) %collective-permute-start.3) | collective-permute-done | bytes 1048608 | tf_op jit(solution)/shard_map/ppermute | solution.py:187
  36.1 5.6 %collective-permute-start.4 = (f32[8,8,32,128]{3,2,1,0:T(8,128)S(1)}, f32[8,8,32,128]{3,2,1,0:T(8,128)S(1)}, u32[]{:S(2)}, u32[]{:S(2)}) collective-permute-start(f32[8,8,32,128]{3,2,1,0:T(8,128)S(1)} %add.18), channel_id=1, source_target_pairs={{0,22},{1,3},{2,0},{3,5},{4,2},{5,7},{6,4},{7,9},{8,6},{9,11},{10,... | collective-permute-start | bytes 3145736 | tf_op jit(solution)/shard_map/ppermute | solution.py:187
  41.7 0.0 collective-permute-done
  41.7 1.6 %add_add_fusion = f32[8,8,32,128]{3,2,1,0:T(8,128)S(1)} fusion(f32[8,8,32,128]{3,2,1,0:T(8,128)} %collective-permute-done.3, f32[8,8,32,128]{3,2,1,0:T(8,128)S(1)} %get-tuple-element.22, f32[8,8,32,128]{3,2,1,0:T(8,128)S(1)} %collective-permute-done), kind=kLoop, calls=%fused_computation | loop fusion | flops 524288 | bytes 4194304 | tf_op jit(solution)/shard_map/add | solution.py:219
  43.3 10.7 %collective-permute-done.4 = f32[8,8,32,128]{3,2,1,0:T(8,128)S(1)} collective-permute-done((f32[8,8,32,128]{3,2,1,0:T(8,128)S(1)}, f32[8,8,32,128]{3,2,1,0:T(8,128)S(1)}, u32[]{:S(2)}, u32[]{:S(2)}) %collective-permute-start.4) | collective-permute-done | bytes 1048608 | tf_op jit(solution)/shard_map/ppermute | solution.py:187
  54.0 1.2 add.21
  55.2 0.0 all-to-all-done.state_ref
  55.2 12.2 %all-to-all-start.1 = ((f32[8,8,32,128]{3,2,1,0:T(8,128)}), f32[8,8,32,128]{3,2,1,0:T(8,128)S(1)}, u32[]{:S(2)}, u32[]{:S(2)}) async-start(f32[8,8,32,128]{3,2,1,0:T(8,128)} %add.21), calls=%async_computation.1 | async-start | bytes 2097152 | tf_op jit(solution)/shard_map/all_to_all | solution.py:221
  67.4 0.1 slice_reduce_fusion
  67.5 0.1 select_reduce_fusion
  67.6 47.3 %all-to-all-done.1.parts_ref = f32[8,8,32,128]{3,2,1,0:T(8,128)S(1)} async-done(((f32[8,8,32,128]{3,2,1,0:T(8,128)}), f32[8,8,32,128]{3,2,1,0:T(8,128)S(1)}, u32[]{:S(2)}, u32[]{:S(2)}) %all-to-all-start.1) | async-done | bytes 1048608 | tf_op jit(solution)/shard_map/all_to_all | solution.py:221
  115.0 1.3 pack_sum.1
  116.3 5.8 %all-to-all-start.2 = ((f32[16,32,128]{2,1,0:T(8,128)}), f32[16,32,128]{2,1,0:T(8,128)S(1)}, u32[]{:S(2)}, u32[]{:S(2)}) async-start(f32[16,32,128]{2,1,0:T(8,128)} %pack_sum.1), calls=%async_computation.2 | async-start | bytes 524288 | tf_op jit(solution)/shard_map/all_to_all | solution.py:223
  122.1 0.2 slice_reduce_fusion.1.loads_ref
  122.2 0.6 iota_reduce_fusion
  122.9 0.1 slice_convert_fusion.chan_ref
  123.0 9.8 %all-to-all-done.2.grad_ref = f32[16,32,128]{2,1,0:T(8,128)S(1)} async-done(((f32[16,32,128]{2,1,0:T(8,128)}), f32[16,32,128]{2,1,0:T(8,128)S(1)}, u32[]{:S(2)}, u32[]{:S(2)}) %all-to-all-start.2) | async-done | bytes 262176 | tf_op jit(solution)/shard_map/all_to_all | solution.py:223
  132.7 1.8 %adam_quantize.1 = (f32[8,32,128]{2,1,0:T(8,128)}, f32[8,32,128]{2,1,0:T(8,128)}, f32[8,32,128]{2,1,0:T(8,128)}, bf16[8,4096]{1,0:T(8,128)(2,1)}, f32[8,32]{1,0:T(8,128)}, /*index=5*/bf16[8,16]{1,0:T(8,128)(2,1)}) custom-call(s32[8]{0:T(128)S(1)} %get-tuple-element.21.src_ref, f32[8]{0:T(128)S(1)} %slice_reduce_fusion.1.loads_ref, ...), custom_call_target="tpu_custom_call" | custom-call | tf_op jit(solution)/shard_map/adam_quantize/pallas_call | solution.py:165
  (5 shorter events, 0.0 us)
Async XLA Ops:
  0.7 1.9 %copy-start = (bf16[1,8,48,4096]{3,2,1,0:T(8,128)(2,1)S(1)}, bf16[1,8,48,4096]{3,2,1,0:T(8,128)(2,1)}, u32[]{:S(2)}) copy-start(bf16[1,8,48,4096]{3,2,1,0:T(8,128)(2,1)} %g_ref.1) | copy-start | bytes 9437188
  2.6 14.1 %copy-start.4 = (s32[8]{0:T(128)S(1)}, s32[8]{0:T(128)}, u32[]{:S(2)}) copy-start(s32[8]{0:T(128)} %dest_ref.3) | copy-start | bytes 100
  2.6 14.2 %copy-start.7 = (s32[8]{0:T(128)S(1)}, s32[8]{0:T(128)}, u32[]{:S(2)}) copy-start(s32[8]{0:T(128)} %param.11) | copy-start | bytes 100
  2.6 14.3 %copy-start.6 = (s32[8,16]{1,0:T(8,128)S(1)}, s32[8,16]{1,0:T(8,128)}, u32[]{:S(2)}) copy-start(s32[8,16]{1,0:T(8,128)} %param.12) | copy-start | bytes 1540
  2.6 14.4 %copy-start.1 = (f32[8,1,4096]{2,1,0:T(1,128)S(1)}, f32[8,1,4096]{2,1,0:T(1,128)}, u32[]{:S(2)}) copy-start(f32[8,1,4096]{2,1,0:T(1,128)} %param.8) | copy-start | bytes 393220
  2.6 14.4 %copy-start.2 = (f32[8,1,4096]{2,1,0:T(1,128)S(1)}, f32[8,1,4096]{2,1,0:T(1,128)}, u32[]{:S(2)}) copy-start(f32[8,1,4096]{2,1,0:T(1,128)} %param.9) | copy-start | bytes 393220
  2.6 14.4 %copy-start.3 = (f32[8,1,4096]{2,1,0:T(1,128)S(1)}, f32[8,1,4096]{2,1,0:T(1,128)}, u32[]{:S(2)}) copy-start(f32[8,1,4096]{2,1,0:T(1,128)} %param.10) | copy-start | bytes 393220
  6.7 5.8 %copy-start.5 = (f32[8,8,32,128]{3,2,1,0:T(8,128)}, f32[8,8,32,128]{3,2,1,0:T(8,128)S(1)}, u32[]{:S(2)}) copy-start(f32[8,8,32,128]{3,2,1,0:T(8,128)S(1)} %get-tuple-element.23) | copy-start | bytes 3145732
  6.7 4.5 %collective-permute-start.2 = (f32[8,8,32,128]{3,2,1,0:T(8,128)S(1)}, f32[8,8,32,128]{3,2,1,0:T(8,128)S(1)}, u32[]{:S(2)}, u32[]{:S(2)}) collective-permute-start(f32[8,8,32,128]{3,2,1,0:T(8,128)S(1)} %get-tuple-element.27), channel_id=1, source_target_pairs={{0,1},{1,0},{2,3},{3,2},{4,5},{5,4},{6,7},{7,6},{8,9},{9,8},{10,11... | collective-permute-start | bytes 3145736 | tf_op jit(solution)/shard_map/ppermute | solution.py:194
  8.6 21.7 %collective-permute-start.1 = (f32[8,8,32,128]{3,2,1,0:T(8,128)}, f32[8,8,32,128]{3,2,1,0:T(8,128)}, u32[]{:S(2)}, u32[]{:S(2)}) collective-permute-start(f32[8,8,32,128]{3,2,1,0:T(8,128)} %get-tuple-element.25), channel_id=1, source_target_pairs={{0,1},{1,0},{2,3},{3,2},{4,5},{5,4},{6,7},{7,6},{8,9},{9,8},{10,11... | collective-permute-start | bytes 3145736 | tf_op jit(solution)/shard_map/ppermute | solution.py:195
  12.5 23.6 %collective-permute-start.3 = (f32[8,8,32,128]{3,2,1,0:T(8,128)}, f32[8,8,32,128]{3,2,1,0:T(8,128)}, u32[]{:S(2)}, u32[]{:S(2)}) collective-permute-start(f32[8,8,32,128]{3,2,1,0:T(8,128)} %add.19), channel_id=1, source_target_pairs={{0,2},{1,23},{2,4},{3,1},{4,6},{5,3},{6,8},{7,5},{8,10},{9,7},{10,... | collective-permute-start | bytes 3145736 | tf_op jit(solution)/shard_map/ppermute | solution.py:187
  18.6 36.6 %all-to-all-start = ((f32[16,104,128]{2,1,0:T(8,128)}), f32[16,104,128]{2,1,0:T(8,128)S(1)}, u32[]{:S(2)}, u32[]{:S(2)}) async-start(f32[16,104,128]{2,1,0:T(8,128)} %pack_state.1), calls=%async_computation | async-start | bytes 1703936 | tf_op jit(solution)/shard_map/all_to_all | solution.py:209
  26.0 15.6 %collective-permute-start = (f32[8,8,32,128]{3,2,1,0:T(8,128)}, f32[8,8,32,128]{3,2,1,0:T(8,128)S(1)}, u32[]{:S(2)}, u32[]{:S(2)}) collective-permute-start(f32[8,8,32,128]{3,2,1,0:T(8,128)} %copy-done.5), channel_id=1, source_target_pairs={{0,1},{1,0},{2,3},{3,2},{4,5},{5,4},{6,7},{7,6},{8,9},{9,8},{10,11... | collective-permute-start | bytes 3145736 | tf_op jit(solution)/shard_map/ppermute | solution.py:196
  36.1 17.9 %collective-permute-start.4 = (f32[8,8,32,128]{3,2,1,0:T(8,128)S(1)}, f32[8,8,32,128]{3,2,1,0:T(8,128)S(1)}, u32[]{:S(2)}, u32[]{:S(2)}) collective-permute-start(f32[8,8,32,128]{3,2,1,0:T(8,128)S(1)} %add.18), channel_id=1, source_target_pairs={{0,22},{1,3},{2,0},{3,5},{4,2},{5,7},{6,4},{7,9},{8,6},{9,11},{10,... | collective-permute-start | bytes 3145736 | tf_op jit(solution)/shard_map/ppermute | solution.py:187
  55.2 59.8 %all-to-all-start.1 = ((f32[8,8,32,128]{3,2,1,0:T(8,128)}), f32[8,8,32,128]{3,2,1,0:T(8,128)S(1)}, u32[]{:S(2)}, u32[]{:S(2)}) async-start(f32[8,8,32,128]{3,2,1,0:T(8,128)} %add.21), calls=%async_computation.1 | async-start | bytes 2097152 | tf_op jit(solution)/shard_map/all_to_all | solution.py:221
  116.3 16.5 %all-to-all-start.2 = ((f32[16,32,128]{2,1,0:T(8,128)}), f32[16,32,128]{2,1,0:T(8,128)S(1)}, u32[]{:S(2)}, u32[]{:S(2)}) async-start(f32[16,32,128]{2,1,0:T(8,128)} %pack_sum.1), calls=%async_computation.2 | async-start | bytes 524288 | tf_op jit(solution)/shard_map/all_to_all | solution.py:223

commit v4 on v3

--- a/solution.py
+++ b/solution.py
@@ -44,12 +44,13 @@
     behind = jnp.where(core == 0, minus, plus)
     other = 1 - core
     for i in range(8):
-        ahead_ref[i] = rows_ref[6 * i + 2 * ahead + core]
-        behind_ref[i] = rows_ref[6 * i + 2 * behind + core]
-        mine_ref[i] = rows_ref[6 * i + 2 * step + core]
-        first_ref[i] = rows_ref[6 * i + 2 * behind + other]
-        next_ref[i] = rows_ref[6 * i + 2 * ahead + other]
-        last_ref[i] = rows_ref[6 * i + 2 * step + other]
+        row = 6 * (4 * (i % 2) + i // 2)
+        ahead_ref[i] = rows_ref[row + 2 * ahead + core]
+        behind_ref[i] = rows_ref[row + 2 * behind + core]
+        mine_ref[i] = rows_ref[row + 2 * step + core]
+        first_ref[i] = rows_ref[row + 2 * behind + other]
+        next_ref[i] = rows_ref[row + 2 * ahead + other]
+        last_ref[i] = rows_ref[row + 2 * step + other]
 
 
 def split(gradients, where):
@@ -218,7 +219,7 @@
 
     partial = lax.optimization_barrier(mine + last + from_first)
     total = partial + from_second
-    parts = lax.all_to_all(total, ("h", "m"), split_axis=0, concat_axis=0, tiled=True)
+    parts = lax.all_to_all(total, ("m", "h"), split_axis=0, concat_axis=0, tiled=True)
     grad = pack_sum(destination, parts)
     grad = lax.all_to_all(grad, ("x", "y"), split_axis=0, concat_axis=0, tiled=True)
     w, m, v, codes, scales, outliers = finish(sources, loads_here, channels_here, grad, state)

time: 135 us -> 129 us (0.956)
  the two profiles are of different devices: /device:TPU:64 before, /device:TPU:160 now
where the time goes in v4:
time: 129 us
  waiting for transfers between devices  71.4 us (55%)
  starting transfers between devices  38.7 us (30%)
  Pallas kernels  8.71 us (7%)
  other arithmetic  6.46 us (5%)
  local copies, waits for them, and re-layouts  2.39 us (2%)
    all_to_all x1, waiting for transfers between devices, body(): lax.all_to_all(total, ('m', 'h'), split_axis=0, concat_axis=0, tiled=True)  44.5 us
    ppermute x2, waiting for transfers between devices, both_ways(): return lax.ppermute(array, Z, pairs)  17.3 us
    all_to_all x1, starting transfers between devices, body(): lax.all_to_all(total, ('m', 'h'), split_axis=0, concat_axis=0, tiled=True)  17.3 us
    all_to_all x1, waiting for transfers between devices, body(): lax.all_to_all(grad, ('x', 'y'), split_axis=0, concat_axis=0, tiled=True)  9.39 us
    ppermute x2, starting transfers between devices, both_ways(): return lax.ppermute(array, Z, pairs)  6.18 us
    all_to_all x1, starting transfers between devices, body(): lax.all_to_all(state, ('x', 'y'), split_axis=0, concat_axis=0, tiled=True)  4.75 us
    all_to_all x1, starting transfers between devices, body(): lax.all_to_all(grad, ('x', 'y'), split_axis=0, concat_axis=0, tiled=True)  4.33 us
    pallas_call x1, Pallas kernels, split(): pl.pallas_call(split_kernel, grid=(steps,), in_specs=[pl.BlockSpec(memory...  4.02 us
  transfers between devices with their start and end apart: 8, of which 5 were waited for; matrix products, arithmetic and copies ran while one was open for 5% of the time, Pallas kernels for 1%

profile of v4, /device:TPU:160, one launch (start us, length us, event | category | flops | bytes accessed | tf_op | source)
XLA Modules:
  0.0 128.5 jit_solution(6968733220317465713)
XLA Ops:
  0.6 0.1 pad_add_fusion.where_ref
  0.7 0.0 copy-start
  0.7 1.9 %copy-done = bf16[1,8,48,4096]{3,2,1,0:T(8,128)(2,1)S(1)} copy-done((bf16[1,8,48,4096]{3,2,1,0:T(8,128)(2,1)S(1)}, bf16[1,8,48,4096]{3,2,1,0:T(8,128)(2,1)}, u32[]{:S(2)}) %copy-start) | copy-done | bytes 3145752
  2.6 0.0 copy-start.4
  2.6 0.0 copy-start.7
  2.6 0.0 copy-start.6
  2.6 0.0 copy-start.1
  2.6 0.0 copy-start.2
  2.6 0.0 copy-start.3
  2.6 4.0 %split_rows.1 = (f32[8,8,32,128]{3,2,1,0:T(8,128)S(1)}, f32[8,8,32,128]{3,2,1,0:T(8,128)S(1)}, f32[8,8,32,128]{3,2,1,0:T(8,128)S(1)}, f32[8,8,32,128]{3,2,1,0:T(...) custom-call(s32[2]{0:T(128)S(1)} %pad_add_fusion.where_ref, bf16[1,8,48,4096]{3,2,1,0:T(8,128)(2,1)S(1)} %copy-done), custom_call_target="tpu_custom_call" | custom-call | tf_op jit(solution)/shard_map/split_rows/pallas_call | solution.py:58
  6.7 1.9 %collective-permute-start.2 = (f32[8,8,32,128]{3,2,1,0:T(8,128)S(1)}, f32[8,8,32,128]{3,2,1,0:T(8,128)S(1)}, u32[]{:S(2)}, u32[]{:S(2)}) collective-permute-start(f32[8,8,32,128]{3,2,1,0:T(8,128)S(1)} %get-tuple-element.27), channel_id=1, source_target_pairs={{0,1},{1,0},{2,3},{3,2},{4,5},{5,4},{6,7},{7,6},{8,9},{9,8},{10,11... | collective-permute-start | bytes 3145736 | tf_op jit(solution)/shard_map/ppermute | solution.py:195
  8.6 2.4 %collective-permute-start.1 = (f32[8,8,32,128]{3,2,1,0:T(8,128)}, f32[8,8,32,128]{3,2,1,0:T(8,128)}, u32[]{:S(2)}, u32[]{:S(2)}) collective-permute-start(f32[8,8,32,128]{3,2,1,0:T(8,128)} %get-tuple-element.25), channel_id=1, source_target_pairs={{0,1},{1,0},{2,3},{3,2},{4,5},{5,4},{6,7},{7,6},{8,9},{9,8},{10,11... | collective-permute-start | bytes 3145736 | tf_op jit(solution)/shard_map/ppermute | solution.py:196
  11.0 0.2 collective-permute-done.2
  11.2 1.2 add.19
  12.5 0.0 copy-done.5
  12.5 4.3 %collective-permute-start.3 = (f32[8,8,32,128]{3,2,1,0:T(8,128)}, f32[8,8,32,128]{3,2,1,0:T(8,128)}, u32[]{:S(2)}, u32[]{:S(2)}) collective-permute-start(f32[8,8,32,128]{3,2,1,0:T(8,128)} %add.19), channel_id=1, source_target_pairs={{0,2},{1,23},{2,4},{3,1},{4,6},{5,3},{6,8},{7,5},{8,10},{9,7},{10,... | collective-permute-start | bytes 3145736 | tf_op jit(solution)/shard_map/ppermute | solution.py:188
  16.7 0.0 copy-done.4
  16.8 0.1 copy.25
  16.8 0.0 copy-done.7
  16.8 0.1 copy.26
  16.9 0.0 copy-done.6
  16.9 0.1 add_convert_fusion
  17.0 0.0 copy-done.1
  17.0 0.0 copy-done.2
  17.0 0.0 copy-done.3
  17.0 1.6 %pack_state.1 = f32[16,104,128]{2,1,0:T(8,128)} custom-call(s32[8]{0:T(128)S(1)} %copy-done.4, f32[8,32,128]{2,1,0:T(8,128)S(1)} %bitcast.17, f32[8,32,128]{2,1,0:T(8,128)S(1)} %bitcast.18, f32[8,32,128]{2,1,0:T(8,128)S(1)} %bitcast.19, f32[8,128]{1,0:T(8,128)S(1)} %pad.4.meta_ref), custom_call_target="tpu_custom_call" | custom-call | tf_op jit(solution)/shard_map/pack_state/pallas_call | solution.py:84
  18.6 4.7 %all-to-all-start = ((f32[16,104,128]{2,1,0:T(8,128)}), f32[16,104,128]{2,1,0:T(8,128)S(1)}, u32[]{:S(2)}, u32[]{:S(2)}) async-start(f32[16,104,128]{2,1,0:T(8,128)} %pack_state.1), calls=%async_computation | async-start | bytes 1703936 | tf_op jit(solution)/shard_map/all_to_all | solution.py:210
  23.3 1.9 %collective-permute-start = (f32[8,8,32,128]{3,2,1,0:T(8,128)}, f32[8,8,32,128]{3,2,1,0:T(8,128)S(1)}, u32[]{:S(2)}, u32[]{:S(2)}) collective-permute-start(f32[8,8,32,128]{3,2,1,0:T(8,128)} %copy-done.5), channel_id=1, source_target_pairs={{0,1},{1,0},{2,3},{3,2},{4,5},{5,4},{6,7},{7,6},{8,9},{9,8},{10,11... | collective-permute-start | bytes 3145736 | tf_op jit(solution)/shard_map/ppermute | solution.py:197
  25.3 0.0 collective-permute-done.1
  25.3 1.5 %add.18 = f32[8,8,32,128]{3,2,1,0:T(8,128)S(1)} add(f32[8,8,32,128]{3,2,1,0:T(8,128)S(1)} %get-tuple-element.24, f32[8,8,32,128]{3,2,1,0:T(8,128)} %collective-permute-done.1) | non-fusion elementwise | flops 262144 | bytes 3145728 | tf_op jit(solution)/shard_map/add | solution.py:199
  26.8 2.7 %collective-permute-done.3 = f32[8,8,32,128]{3,2,1,0:T(8,128)} collective-permute-done((f32[8,8,32,128]{3,2,1,0:T(8,128)}, f32[8,8,32,128]{3,2,1,0:T(8,128)}, u32[]{:S(2)}, u32[]{:S(2)}) %collective-permute-start.3) | collective-permute-done | bytes 1048608 | tf_op jit(solution)/shard_map/ppermute | solution.py:188
  29.5 1.9 %collective-permute-start.4 = (f32[8,8,32,128]{3,2,1,0:T(8,128)S(1)}, f32[8,8,32,128]{3,2,1,0:T(8,128)S(1)}, u32[]{:S(2)}, u32[]{:S(2)}) collective-permute-start(f32[8,8,32,128]{3,2,1,0:T(8,128)S(1)} %add.18), channel_id=1, source_target_pairs={{0,22},{1,3},{2,0},{3,5},{4,2},{5,7},{6,4},{7,9},{8,6},{9,11},{10,... | collective-permute-start | bytes 3145736 | tf_op jit(solution)/shard_map/ppermute | solution.py:188
  31.4 0.0 collective-permute-done
  31.4 1.6 %add_add_fusion = f32[8,8,32,128]{3,2,1,0:T(8,128)S(1)} fusion(f32[8,8,32,128]{3,2,1,0:T(8,128)} %collective-permute-done.3, f32[8,8,32,128]{3,2,1,0:T(8,128)S(1)} %get-tuple-element.22, f32[8,8,32,128]{3,2,1,0:T(8,128)S(1)} %collective-permute-done), kind=kLoop, calls=%fused_computation | loop fusion | flops 524288 | bytes 4194304 | tf_op jit(solution)/shard_map/add | solution.py:220
  33.0 14.6 %collective-permute-done.4 = f32[8,8,32,128]{3,2,1,0:T(8,128)S(1)} collective-permute-done((f32[8,8,32,128]{3,2,1,0:T(8,128)S(1)}, f32[8,8,32,128]{3,2,1,0:T(8,128)S(1)}, u32[]{:S(2)}, u32[]{:S(2)}) %collective-permute-start.4) | collective-permute-done | bytes 1048608 | tf_op jit(solution)/shard_map/ppermute | solution.py:188
  47.6 1.2 add.21
  48.8 0.0 all-to-all-done.state_ref
  48.8 17.3 %all-to-all-start.1 = ((f32[8,8,32,128]{3,2,1,0:T(8,128)}), f32[8,8,32,128]{3,2,1,0:T(8,128)S(1)}, u32[]{:S(2)}, u32[]{:S(2)}) async-start(f32[8,8,32,128]{3,2,1,0:T(8,128)} %add.21), calls=%async_computation.1 | async-start | bytes 2097152 | tf_op jit(solution)/shard_map/all_to_all | solution.py:222
  66.0 0.1 slice_reduce_fusion
  66.2 0.1 select_reduce_fusion
  66.3 44.5 %all-to-all-done.1.parts_ref = f32[8,8,32,128]{3,2,1,0:T(8,128)S(1)} async-done(((f32[8,8,32,128]{3,2,1,0:T(8,128)}), f32[8,8,32,128]{3,2,1,0:T(8,128)S(1)}, u32[]{:S(2)}, u32[]{:S(2)}) %all-to-all-start.1) | async-done | bytes 1048608 | tf_op jit(solution)/shard_map/all_to_all | solution.py:222
  110.8 1.3 pack_sum.1
  112.1 4.3 %all-to-all-start.2 = ((f32[16,32,128]{2,1,0:T(8,128)}), f32[16,32,128]{2,1,0:T(8,128)S(1)}, u32[]{:S(2)}, u32[]{:S(2)}) async-start(f32[16,32,128]{2,1,0:T(8,128)} %pack_sum.1), calls=%async_computation.2 | async-start | bytes 524288 | tf_op jit(solution)/shard_map/all_to_all | solution.py:224
  116.4 0.2 slice_reduce_fusion.1.loads_ref
  116.6 0.6 iota_reduce_fusion
  117.2 0.1 slice_convert_fusion.chan_ref
  117.3 9.4 %all-to-all-done.2.grad_ref = f32[16,32,128]{2,1,0:T(8,128)S(1)} async-done(((f32[16,32,128]{2,1,0:T(8,128)}), f32[16,32,128]{2,1,0:T(8,128)S(1)}, u32[]{:S(2)}, u32[]{:S(2)}) %all-to-all-start.2) | async-done | bytes 262176 | tf_op jit(solution)/shard_map/all_to_all | solution.py:224
  126.7 1.8 %adam_quantize.1 = (f32[8,32,128]{2,1,0:T(8,128)}, f32[8,32,128]{2,1,0:T(8,128)}, f32[8,32,128]{2,1,0:T(8,128)}, bf16[8,4096]{1,0:T(8,128)(2,1)}, f32[8,32]{1,0:T(8,128)}, /*index=5*/bf16[8,16]{1,0:T(8,128)(2,1)}) custom-call(s32[8]{0:T(128)S(1)} %get-tuple-element.21.src_ref, f32[8]{0:T(128)S(1)} %slice_reduce_fusion.1.loads_ref, ...), custom_call_target="tpu_custom_call" | custom-call | tf_op jit(solution)/shard_map/adam_quantize/pallas_call | solution.py:166
  (5 shorter events, 0.0 us)
Async XLA Ops:
  0.7 1.9 %copy-start = (bf16[1,8,48,4096]{3,2,1,0:T(8,128)(2,1)S(1)}, bf16[1,8,48,4096]{3,2,1,0:T(8,128)(2,1)}, u32[]{:S(2)}) copy-start(bf16[1,8,48,4096]{3,2,1,0:T(8,128)(2,1)} %g_ref.1) | copy-start | bytes 9437188
  2.6 14.1 %copy-start.4 = (s32[8]{0:T(128)S(1)}, s32[8]{0:T(128)}, u32[]{:S(2)}) copy-start(s32[8]{0:T(128)} %dest_ref.3) | copy-start | bytes 100
  2.6 14.2 %copy-start.7 = (s32[8]{0:T(128)S(1)}, s32[8]{0:T(128)}, u32[]{:S(2)}) copy-start(s32[8]{0:T(128)} %param.11) | copy-start | bytes 100
  2.6 14.3 %copy-start.6 = (s32[8,16]{1,0:T(8,128)S(1)}, s32[8,16]{1,0:T(8,128)}, u32[]{:S(2)}) copy-start(s32[8,16]{1,0:T(8,128)} %param.12) | copy-start | bytes 1540
  2.6 14.4 %copy-start.1 = (f32[8,1,4096]{2,1,0:T(1,128)S(1)}, f32[8,1,4096]{2,1,0:T(1,128)}, u32[]{:S(2)}) copy-start(f32[8,1,4096]{2,1,0:T(1,128)} %param.8) | copy-start | bytes 393220
  2.6 14.4 %copy-start.2 = (f32[8,1,4096]{2,1,0:T(1,128)S(1)}, f32[8,1,4096]{2,1,0:T(1,128)}, u32[]{:S(2)}) copy-start(f32[8,1,4096]{2,1,0:T(1,128)} %param.9) | copy-start | bytes 393220
  2.6 14.4 %copy-start.3 = (f32[8,1,4096]{2,1,0:T(1,128)S(1)}, f32[8,1,4096]{2,1,0:T(1,128)}, u32[]{:S(2)}) copy-start(f32[8,1,4096]{2,1,0:T(1,128)} %param.10) | copy-start | bytes 393220
  6.7 5.8 %copy-start.5 = (f32[8,8,32,128]{3,2,1,0:T(8,128)}, f32[8,8,32,128]{3,2,1,0:T(8,128)S(1)}, u32[]{:S(2)}) copy-start(f32[8,8,32,128]{3,2,1,0:T(8,128)S(1)} %get-tuple-element.23) | copy-start | bytes 3145732
  6.7 4.5 %collective-permute-start.2 = (f32[8,8,32,128]{3,2,1,0:T(8,128)S(1)}, f32[8,8,32,128]{3,2,1,0:T(8,128)S(1)}, u32[]{:S(2)}, u32[]{:S(2)}) collective-permute-start(f32[8,8,32,128]{3,2,1,0:T(8,128)S(1)} %get-tuple-element.27), channel_id=1, source_target_pairs={{0,1},{1,0},{2,3},{3,2},{4,5},{5,4},{6,7},{7,6},{8,9},{9,8},{10,11... | collective-permute-start | bytes 3145736 | tf_op jit(solution)/shard_map/ppermute | solution.py:195
  8.6 16.7 %collective-permute-start.1 = (f32[8,8,32,128]{3,2,1,0:T(8,128)}, f32[8,8,32,128]{3,2,1,0:T(8,128)}, u32[]{:S(2)}, u32[]{:S(2)}) collective-permute-start(f32[8,8,32,128]{3,2,1,0:T(8,128)} %get-tuple-element.25), channel_id=1, source_target_pairs={{0,1},{1,0},{2,3},{3,2},{4,5},{5,4},{6,7},{7,6},{8,9},{9,8},{10,11... | collective-permute-start | bytes 3145736 | tf_op jit(solution)/shard_map/ppermute | solution.py:196
  12.5 17.0 %collective-permute-start.3 = (f32[8,8,32,128]{3,2,1,0:T(8,128)}, f32[8,8,32,128]{3,2,1,0:T(8,128)}, u32[]{:S(2)}, u32[]{:S(2)}) collective-permute-start(f32[8,8,32,128]{3,2,1,0:T(8,128)} %add.19), channel_id=1, source_target_pairs={{0,2},{1,23},{2,4},{3,1},{4,6},{5,3},{6,8},{7,5},{8,10},{9,7},{10,... | collective-permute-start | bytes 3145736 | tf_op jit(solution)/shard_map/ppermute | solution.py:188
  18.6 30.2 %all-to-all-start = ((f32[16,104,128]{2,1,0:T(8,128)}), f32[16,104,128]{2,1,0:T(8,128)S(1)}, u32[]{:S(2)}, u32[]{:S(2)}) async-start(f32[16,104,128]{2,1,0:T(8,128)} %pack_state.1), calls=%async_computation | async-start | bytes 1703936 | tf_op jit(solution)/shard_map/all_to_all | solution.py:210
  23.3 8.0 %collective-permute-start = (f32[8,8,32,128]{3,2,1,0:T(8,128)}, f32[8,8,32,128]{3,2,1,0:T(8,128)S(1)}, u32[]{:S(2)}, u32[]{:S(2)}) collective-permute-start(f32[8,8,32,128]{3,2,1,0:T(8,128)} %copy-done.5), channel_id=1, source_target_pairs={{0,1},{1,0},{2,3},{3,2},{4,5},{5,4},{6,7},{7,6},{8,9},{9,8},{10,11... | collective-permute-start | bytes 3145736 | tf_op jit(solution)/shard_map/ppermute | solution.py:197
  29.5 18.1 %collective-permute-start.4 = (f32[8,8,32,128]{3,2,1,0:T(8,128)S(1)}, f32[8,8,32,128]{3,2,1,0:T(8,128)S(1)}, u32[]{:S(2)}, u32[]{:S(2)}) collective-permute-start(f32[8,8,32,128]{3,2,1,0:T(8,128)S(1)} %add.18), channel_id=1, source_target_pairs={{0,22},{1,3},{2,0},{3,5},{4,2},{5,7},{6,4},{7,9},{8,6},{9,11},{10,... | collective-permute-start | bytes 3145736 | tf_op jit(solution)/shard_map/ppermute | solution.py:188
  48.8 62.0 %all-to-all-start.1 = ((f32[8,8,32,128]{3,2,1,0:T(8,128)}), f32[8,8,32,128]{3,2,1,0:T(8,128)S(1)}, u32[]{:S(2)}, u32[]{:S(2)}) async-start(f32[8,8,32,128]{3,2,1,0:T(8,128)} %add.21), calls=%async_computation.1 | async-start | bytes 2097152 | tf_op jit(solution)/shard_map/all_to_all | solution.py:222
  112.1 14.6 %all-to-all-start.2 = ((f32[16,32,128]{2,1,0:T(8,128)}), f32[16,32,128]{2,1,0:T(8,128)S(1)}, u32[]{:S(2)}, u32[]{:S(2)}) async-start(f32[16,32,128]{2,1,0:T(8,128)} %pack_sum.1), calls=%async_computation.2 | async-start | bytes 524288 | tf_op jit(solution)/shard_map/all_to_all | solution.py:224
